TPU v7x, 256 devices: a whole 4x4x8 slice. The times are simulated.
256 devices in a mesh: seq: 32 (over y, z_hi, x), tower: 8 (over z_lo, core).
Axes of the slice: x: 4, y: 4, z: 8 (z_hi: 2, z_lo: 4; z = z_hi * 4 + z_lo), core: 2. Of those that a mesh axis runs over, the one named last changes fastest.
Arguments:
- q_self: bfloat16 [8, 3072, 3072], P('tower', 'seq'), may hold values from -6 to 6
- k_self: bfloat16 [8, 3072, 3072], P('tower', 'seq'), may hold values from -6 to 6
- v_self: bfloat16 [8, 3072, 3072], P('tower', 'seq'), may hold values from -6 to 6
- q_cross: bfloat16 [8, 3072, 3072], P('tower', 'seq'), may hold values from -12 to 12
- k_cross: bfloat16 [8, 3072, 3072], P('tower', 'seq'), may hold values from -8 to 8
- v_cross: bfloat16 [8, 3072, 3072], P('tower', 'seq'), may hold values from -8 to 8
- scale_exps: int32 [8, 2, 24], P('tower'), may hold values from -8 to -5
- cross_slopes: float32 [2, 24], replicated, may hold values from 0.5 to 16
- offsets: int32 [8], replicated, may hold values from 0 to 1535
Outputs:
- self_out: bfloat16 [8, 3072, 3072], P('tower', 'seq')
- cross_out: bfloat16 [8, 3072, 3072], P('tower', 'seq')
All inputs are finite; a program needn't handle non-finite values.
Results may differ from a plain program's by a relative error of at most 0.0049.
Values may be sent and summed in bfloat16 or wider, within the bound.
No kernel may reach another device: no remote copies, remote signals or barrier semaphores. Data moves between devices by JAX's collectives and lax.ppermute only.
A program may use at most 64 MiB of HBM per device.

v0:
```python
import math

import jax
import jax.numpy as jnp
from jax import lax
from jax.sharding import PartitionSpec as P

HEADS = 24
HD = 128


clip_top = 448.0


def swapped(block, axis, stride):
    count = lax.axis_size(axis)
    route = []
    for low in range(count):
        high = low | 1 << stride
        if high != low and high < count:
            route += [(low, high), (high, low)]
    return lax.ppermute(block, axis, route)


def key_layout(matrix, groups, part_count):
    row_count, heads_all, head_width = matrix.shape
    per_group = heads_all // groups
    blocks = matrix.reshape(row_count, groups, per_group, head_width).transpose(1, 0, 2, 3)
    blocks = jnp.broadcast_to(
        blocks[:, None], (groups, part_count, row_count, per_group, head_width)
    )
    return blocks.reshape(groups * part_count, row_count, per_group, head_width)


def query_layout(matrix, groups, part_count):
    row_count, heads_all, head_width = matrix.shape
    per_group = heads_all // groups
    share_rows = row_count // part_count
    blocks = matrix.reshape(part_count, share_rows, groups, per_group, head_width).transpose(
        2, 0, 1, 3, 4
    )
    return blocks.reshape(groups * part_count, share_rows, per_group, head_width)


def token_layout(replies, groups, part_count):
    senders, share_rows, per_group, head_width = replies.shape
    blocks = replies.reshape(groups, part_count, share_rows, per_group, head_width).transpose(
        1, 2, 0, 3, 4
    )
    return blocks.reshape(1, part_count * share_rows, groups * per_group * head_width)


def attend(queries, key_rows, value_rows, slope_rates, query_time, key_time, tokens_all):
    query_count, per_group, head_width = queries.shape
    inv_root = head_width ** (-0.5)

    def one_head(head_index):
        head_queries = lax.dynamic_index_in_dim(queries, head_index, 1, keepdims=False)
        head_keys = lax.dynamic_index_in_dim(key_rows, head_index, 1, keepdims=False)
        head_values = lax.dynamic_index_in_dim(value_rows, head_index, 1, keepdims=False)

        def one_block(start_row):
            scores = (
                jnp.dot(head_queries, head_keys.T, preferred_element_type=jnp.float32) * inv_root
            )
            if slope_rates is not None:
                distance = jnp.abs(query_time[:, None] - key_time[None, :]).astype(jnp.float32)
                scores = scores - slope_rates[head_index] * (distance / tokens_all)
            row_peak = jnp.max(scores, axis=1, keepdims=True)
            lifted = jnp.exp(scores - row_peak)
            weights = (lifted / jnp.sum(lifted, axis=1, keepdims=True)).astype(jnp.bfloat16)
            return jnp.dot(weights, head_values, preferred_element_type=jnp.float32).astype(
                jnp.bfloat16
            )

        outputs = lax.map(
            one_block, jnp.arange(query_count // query_count, dtype=jnp.int32) * query_count
        )
        return outputs.reshape(query_count, head_width)

    return lax.map(one_head, jnp.arange(per_group, dtype=jnp.int32)).transpose(1, 0, 2)


def per_device(
    q_self, k_self, v_self, q_cross, k_cross, v_cross, scale_exps, cross_slopes, offsets
):
    seq_size = lax.axis_size("seq")
    tower_size = lax.axis_size("tower")
    half_count = tower_size // 2
    swap_bit = half_count.bit_length() - 1
    groups = math.gcd(HEADS, seq_size)
    part_count = seq_size // groups
    per_group = HEADS // groups
    row_count = q_self.shape[1]
    share_rows = row_count // part_count
    tokens_all = seq_size * row_count
    seat_index = lax.axis_index("seq")
    tower_index = lax.axis_index("tower")
    partner = jnp.bitwise_xor(tower_index, half_count)
    group_index = seat_index // part_count
    part_index = seat_index % part_count

    def split_heads(matrix):
        return matrix[0].reshape(row_count, HEADS, HD)

    powers = scale_exps[0].astype(jnp.float32)
    shrink = jnp.exp2(-powers)[:, None, :, None]
    key_codes = jnp.clip(
        split_heads(k_cross).astype(jnp.float32) * shrink[0], -clip_top, clip_top
    ).astype(jnp.bfloat16)
    value_codes = jnp.clip(
        split_heads(v_cross).astype(jnp.float32) * shrink[1], -clip_top, clip_top
    ).astype(jnp.bfloat16)
    code_scales = jnp.exp2(powers).astype(jnp.bfloat16)
    mine_queries = query_layout(split_heads(q_self), groups, part_count)
    mine_keys = key_layout(split_heads(k_self), groups, part_count)
    mine_values = key_layout(split_heads(v_self), groups, part_count)
    pair_queries = query_layout(split_heads(q_cross), groups, part_count)
    key_codes, value_codes, code_scales = swapped(
        (key_codes, value_codes, code_scales), "tower", swap_bit
    )
    pair_keys = key_layout(key_codes, groups, part_count)
    pair_values = key_layout(value_codes, groups, part_count)
    self_queries, self_keys, self_values, cross_queries, cross_keys, cross_values = (
        lax.all_to_all(mine_queries, "seq", split_axis=0, concat_axis=1, tiled=True),
        lax.all_to_all(mine_keys, "seq", split_axis=0, concat_axis=1, tiled=True),
        lax.all_to_all(mine_values, "seq", split_axis=0, concat_axis=1, tiled=True),
        lax.all_to_all(pair_queries, "seq", split_axis=0, concat_axis=1, tiled=True),
        lax.all_to_all(pair_keys, "seq", split_axis=0, concat_axis=1, tiled=True),
        lax.all_to_all(pair_values, "seq", split_axis=0, concat_axis=1, tiled=True),
    )
    self_result = attend(
        self_queries[0], self_keys[0], self_values[0], None, None, None, tokens_all
    )
    group_scales = lax.dynamic_slice_in_dim(
        code_scales.astype(jnp.float32), group_index * per_group, per_group, 1
    )
    keys_full = (cross_keys[0].astype(jnp.float32) * group_scales[0][None, :, None]).astype(
        jnp.bfloat16
    )
    values_full = (cross_values[0].astype(jnp.float32) * group_scales[1][None, :, None]).astype(
        jnp.bfloat16
    )
    source_rows = jnp.arange(seq_size, dtype=jnp.int32)[:, None] * row_count
    local_rows = part_index * share_rows + jnp.arange(share_rows, dtype=jnp.int32)[None, :]
    query_time = (source_rows + local_rows).reshape(seq_size * share_rows) + offsets[tower_index]
    key_time = jnp.arange(tokens_all, dtype=jnp.int32) + offsets[partner]
    modality = tower_index // half_count
    slope_row = lax.dynamic_index_in_dim(cross_slopes, modality, 0, keepdims=False)
    slope_rates = lax.dynamic_slice_in_dim(slope_row, group_index * per_group, per_group, 0)
    cross_result = attend(
        cross_queries[0], keys_full, values_full, slope_rates, query_time, key_time, tokens_all
    )
    self_back, cross_back = (
        lax.all_to_all(
            self_result.reshape(seq_size, share_rows, per_group, HD),
            "seq",
            split_axis=0,
            concat_axis=0,
            tiled=True,
        ),
        lax.all_to_all(
            cross_result.reshape(seq_size, share_rows, per_group, HD),
            "seq",
            split_axis=0,
            concat_axis=0,
            tiled=True,
        ),
    )
    return (
        token_layout(self_back, groups, part_count),
        token_layout(cross_back, groups, part_count),
    )


def solution(mesh):
    return jax.shard_map(
        per_device,
        mesh=mesh,
        in_specs=(
            P("tower", "seq", None),
            P("tower", "seq", None),
            P("tower", "seq", None),
            P("tower", "seq", None),
            P("tower", "seq", None),
            P("tower", "seq", None),
            P("tower", None, None),
            P(),
            P(),
        ),
        out_specs=(P("tower", "seq", None), P("tower", "seq", None)),
        check_vma=False,
    )
```

profile of v0, /device:TPU:2, one launch (start us, length us, event | category | flops | bytes accessed | tf_op | source)
XLA Modules:
  0.0 502.6 jit_solution(4804553084871833878)
XLA Ops:
  3.7 14.2 %all-to-all-start.4 = ((bf16[32,24,3,128]{3,1,2,0:T(8,128)(2,1)}), bf16[32,24,3,128]{3,1,2,0:T(8,128)(2,1)S(1)}, u32[]{:S(2)}, u32[]{:S(2)}) async-start(bf16[32,24,3,128]{3,1,2,0:T(8,128)(2,1)} %bitcast.19), calls=%async_computation.4 | async-start | bytes 1179648 | tf_op jit(solution)/shard_map/all_to_all | solution.py:128
  20.8 13.8 %all-to-all-done.4 = bf16[32,24,3,128]{3,1,2,0:T(8,128)(2,1)S(1)} async-done(((bf16[32,24,3,128]{3,1,2,0:T(8,128)(2,1)}), bf16[32,24,3,128]{3,1,2,0:T(8,128)(2,1)S(1)}, u32[]{:S(2)}, u32[]{:S(2)}) %all-to-all-start.4) | async-done | bytes 589856 | tf_op jit(solution)/shard_map/all_to_all | solution.py:128
  34.7 6.1 %all-to-all-start = ((bf16[32,24,3,128]{3,1,2,0:T(8,128)(2,1)}), bf16[32,24,3,128]{3,1,2,0:T(8,128)(2,1)S(1)}, u32[]{:S(2)}, u32[]{:S(2)}) async-start(bf16[32,24,3,128]{3,1,2,0:T(8,128)(2,1)} %bitcast.6), calls=%async_computation | async-start | bytes 1179648 | tf_op jit(solution)/shard_map/all_to_all | solution.py:125
  42.0 12.6 %all-to-all-done = bf16[32,24,3,128]{3,1,2,0:T(8,128)(2,1)S(1)} async-done(((bf16[32,24,3,128]{3,1,2,0:T(8,128)(2,1)}), bf16[32,24,3,128]{3,1,2,0:T(8,128)(2,1)S(1)}, u32[]{:S(2)}, u32[]{:S(2)}) %all-to-all-start) | async-done | bytes 589856 | tf_op jit(solution)/shard_map/all_to_all | solution.py:125
  56.4 8.4 %all-to-all-start.1 = ((bf16[32,96,3,128]{3,1,2,0:T(8,128)(2,1)}), bf16[32,96,3,128]{3,1,2,0:T(8,128)(2,1)S(1)}, u32[]{:S(2)}, u32[]{:S(2)}) async-start(bf16[32,96,3,128]{3,1,2,0:T(8,128)(2,1)} %bitcast.132), calls=%async_computation.1 | async-start | bytes 4718592 | tf_op jit(solution)/shard_map/all_to_all | solution.py:126
  67.7 24.8 %all-to-all-done.1 = bf16[32,96,3,128]{3,1,2,0:T(8,128)(2,1)S(1)} async-done(((bf16[32,96,3,128]{3,1,2,0:T(8,128)(2,1)}), bf16[32,96,3,128]{3,1,2,0:T(8,128)(2,1)S(1)}, u32[]{:S(2)}, u32[]{:S(2)}) %all-to-all-start.1) | async-done | bytes 2359328 | tf_op jit(solution)/shard_map/all_to_all | solution.py:126
  92.5 3.3 broadcast_in_dim.29
  95.8 6.4 %all-to-all-start.2 = ((bf16[32,96,3,128]{3,1,2,0:T(8,128)(2,1)}), bf16[32,96,3,128]{3,1,2,0:T(8,128)(2,1)}, u32[]{:S(2)}, u32[]{:S(2)}) async-start(bf16[32,96,3,128]{3,1,2,0:T(8,128)(2,1)} %bitcast.131), calls=%async_computation.2 | async-start | bytes 4718592 | tf_op jit(solution)/shard_map/all_to_all | solution.py:127
  102.8 63.8 %collective-permute-start.2 = (bf16[96,24,128]{2,1,0:T(8,128)(2,1)S(1)}, bf16[96,24,128]{2,1,0:T(8,128)(2,1)S(1)}, u32[]{:S(2)}, u32[]{:S(2)}) collective-permute-start(bf16[96,24,128]{2,1,0:T(8,128)(2,1)S(1)} %fusion.35), channel_id=1, source_target_pairs={{0,4},{4,0},{1,5},{5,1},{2,6},{6,2},{3,7},{7,3},{8,12},{12,8},{9,1... | collective-permute-start | bytes 1769480 | tf_op jit(solution)/shard_map/ppermute | solution.py:22
  166.6 91.7 %collective-permute-done.2 = bf16[96,24,128]{2,1,0:T(8,128)(2,1)S(1)} collective-permute-done((bf16[96,24,128]{2,1,0:T(8,128)(2,1)S(1)}, bf16[96,24,128]{2,1,0:T(8,128)(2,1)S(1)}, u32[]{:S(2)}, u32[]{:S(2)}) %collective-permute-start.2) | collective-permute-done | bytes 589856 | tf_op jit(solution)/shard_map/ppermute | solution.py:22
  260.2 14.4 %all-to-all-start.6 = ((bf16[32,96,3,128]{3,1,2,0:T(8,128)(2,1)}), bf16[32,96,3,128]{3,1,2,0:T(8,128)(2,1)}, u32[]{:S(2)}, u32[]{:S(2)}) async-start(bf16[32,96,3,128]{3,1,2,0:T(8,128)(2,1)} %bitcast.32), calls=%async_computation.6 | async-start | bytes 4718592 | tf_op jit(solution)/shard_map/all_to_all | solution.py:130
  275.2 3.0 collective-permute-start
  279.5 47.2 %collective-permute-done.1 = bf16[2,24]{1,0:T(2,128)(2,1)S(1)} collective-permute-done((bf16[2,24]{1,0:T(2,128)(2,1)S(1)}, bf16[2,24]{1,0:T(2,128)(2,1)S(1)}, u32[]{:S(2)}, u32[]{:S(2)}) %collective-permute-start.1) | collective-permute-done | bytes 128 | tf_op jit(solution)/shard_map/ppermute | solution.py:22
  327.3 10.6 %collective-permute-done = bf16[96,24,128]{2,1,0:T(8,128)(2,1)S(1)} collective-permute-done((bf16[96,24,128]{2,1,0:T(8,128)(2,1)S(1)}, bf16[96,24,128]{2,1,0:T(8,128)(2,1)S(1)}, u32[]{:S(2)}, u32[]{:S(2)}) %collective-permute-start) | collective-permute-done | bytes 589856 | tf_op jit(solution)/shard_map/ppermute | solution.py:22
  340.8 3.4 copy.66
  346.0 12.6 %all-to-all-start.5 = ((bf16[32,96,3,128]{3,1,2,0:T(8,128)(2,1)}), bf16[32,96,3,128]{3,1,2,0:T(8,128)(2,1)}, u32[]{:S(2)}, u32[]{:S(2)}) async-start(bf16[32,96,3,128]{3,1,2,0:T(8,128)(2,1)} %bitcast.130), calls=%async_computation.5 | async-start | bytes 4718592 | tf_op jit(solution)/shard_map/all_to_all | solution.py:129
  359.3 30.5 %while.21 = (s32[]{:T(128)}, bf16[3,768,128]{2,1,0:T(8,128)(2,1)S(1)}, s32[3]{0:T(128)}, bf16[768,3,128]{2,0,1:T(8,128)(2,1)S(1)}, bf16[3072,3,128]{2,0,1:T(8,12...) while((s32[]{:T(128)}, bf16[3,768,128]{2,1,0:T(8,128)(2,1)S(1)}, ...), condition=%wide.region_3.4_spmd, body=%wide.region_0.3_spmd.sunk | while | flops 1229289984 | bytes 30296720 | solution.py:81
  365.8 3.6 fusion.50
  376.0 3.6 fusion.50
  386.1 3.6 fusion.50
  393.1 23.5 %all-to-all-done.5 = bf16[32,96,3,128]{3,1,2,0:T(8,128)(2,1)} async-done(((bf16[32,96,3,128]{3,1,2,0:T(8,128)(2,1)}), bf16[32,96,3,128]{3,1,2,0:T(8,128)(2,1)}, u32[]{:S(2)}, u32[]{:S(2)}) %all-to-all-start.5) | async-done | bytes 2359328 | tf_op jit(solution)/shard_map/all_to_all | solution.py:129
  416.6 7.0 %all-to-all-start.3 = ((bf16[32,24,3,128]{3,1,2,0:T(8,128)(2,1)}), bf16[32,24,3,128]{3,1,2,0:T(8,128)(2,1)S(1)}, u32[]{:S(2)}, u32[]{:S(2)}) async-start(bf16[32,24,3,128]{3,1,2,0:T(8,128)(2,1)} %copy.67), calls=%async_computation.3 | async-start | bytes 1179648 | tf_op jit(solution)/shard_map/all_to_all | solution.py:155
  425.5 2.0 fusion.33
  428.1 46.1 %while.22 = (s32[]{:T(128)}, bf16[3,768,128]{2,1,0:T(8,128)(2,1)S(1)}, s32[3]{0:T(128)}, bf16[768,3,128]{2,0,1:T(8,128)(2,1)}, bf16[3072,3,128]{2,0,1:T(8,128)(2...) while((s32[]{:T(128)}, ...), condition=%wide.region_7.8_spmd.clone, body=%wide.region_4.7_spmd.clone.sunk | while | flops 1236372480 | bytes 30333892 | solution.py:81
  435.6 4.3 fusion.52
  441.3 2.2 fusion.54
  450.9 4.3 fusion.52
  456.7 2.2 fusion.54
  466.3 4.3 fusion.52
  472.1 2.2 fusion.54
  475.2 12.2 %all-to-all-start.7 = ((bf16[32,24,3,128]{3,1,2,0:T(8,128)(2,1)}), bf16[32,24,3,128]{3,1,2,0:T(8,128)(2,1)S(1)}, u32[]{:S(2)}, u32[]{:S(2)}) async-start(bf16[32,24,3,128]{3,1,2,0:T(8,128)(2,1)} %copy.75), calls=%async_computation.7 | async-start | bytes 1179648 | tf_op jit(solution)/shard_map/all_to_all | solution.py:162
  489.0 12.1 %all-to-all-done.7 = bf16[32,24,3,128]{3,1,2,0:T(8,128)(2,1)S(1)} async-done(((bf16[32,24,3,128]{3,1,2,0:T(8,128)(2,1)}), bf16[32,24,3,128]{3,1,2,0:T(8,128)(2,1)S(1)}, u32[]{:S(2)}, u32[]{:S(2)}) %all-to-all-start.7) | async-done | bytes 589856 | tf_op jit(solution)/shard_map/all_to_all | solution.py:162
  (101 shorter events, 64.6 us)
Async XLA Ops:
  0.6 278.2 %copy-start = (f32[2,24]{1,0:T(2,128)S(1)}, f32[2,24]{1,0:T(2,128)}, u32[]{:S(2)}) copy-start(f32[2,24]{1,0:T(2,128)} %param.20) | copy-start | bytes 580
  0.6 40.2 %copy-start.9 = (bf16[1,96,3072]{2,1,0:T(8,128)(2,1)S(1)}, bf16[1,96,3072]{2,1,0:T(8,128)(2,1)}, u32[]{:S(2)}) copy-start(bf16[1,96,3072]{2,1,0:T(8,128)(2,1)} %param.14) | copy-start | bytes 1769476
  3.7 31.0 %all-to-all-start.4 = ((bf16[32,24,3,128]{3,1,2,0:T(8,128)(2,1)}), bf16[32,24,3,128]{3,1,2,0:T(8,128)(2,1)S(1)}, u32[]{:S(2)}, u32[]{:S(2)}) async-start(bf16[32,24,3,128]{3,1,2,0:T(8,128)(2,1)} %bitcast.19), calls=%async_computation.4 | async-start | bytes 1179648 | tf_op jit(solution)/shard_map/all_to_all | solution.py:128
  34.7 21.7 %copy-start.3 = (bf16[32,24,3,128]{3,1,2,0:T(8,128)(2,1)}, bf16[32,24,3,128]{3,1,2,0:T(8,128)(2,1)S(1)}, u32[]{:S(2)}) copy-start(bf16[32,24,3,128]{3,1,2,0:T(8,128)(2,1)S(1)} %all-to-all-done.4) | copy-start | bytes 1769476
  34.7 19.9 %all-to-all-start = ((bf16[32,24,3,128]{3,1,2,0:T(8,128)(2,1)}), bf16[32,24,3,128]{3,1,2,0:T(8,128)(2,1)S(1)}, u32[]{:S(2)}, u32[]{:S(2)}) async-start(bf16[32,24,3,128]{3,1,2,0:T(8,128)(2,1)} %bitcast.6), calls=%async_computation | async-start | bytes 1179648 | tf_op jit(solution)/shard_map/all_to_all | solution.py:125
  54.6 1.8 copy-start.5
  56.4 36.1 %all-to-all-start.1 = ((bf16[32,96,3,128]{3,1,2,0:T(8,128)(2,1)}), bf16[32,96,3,128]{3,1,2,0:T(8,128)(2,1)S(1)}, u32[]{:S(2)}, u32[]{:S(2)}) async-start(bf16[32,96,3,128]{3,1,2,0:T(8,128)(2,1)} %bitcast.132), calls=%async_computation.1 | async-start | bytes 4718592 | tf_op jit(solution)/shard_map/all_to_all | solution.py:126
  67.7 34.4 %copy-start.7 = (bf16[1,96,3072]{2,1,0:T(8,128)(2,1)S(1)}, bf16[1,96,3072]{2,1,0:T(8,128)(2,1)}, u32[]{:S(2)}) copy-start(bf16[1,96,3072]{2,1,0:T(8,128)(2,1)} %param.18) | copy-start | bytes 1769476
  92.5 9.8 %copy-start.2 = (bf16[32,96,3,128]{3,1,2,0:T(8,128)(2,1)}, bf16[32,96,3,128]{3,1,2,0:T(8,128)(2,1)S(1)}, u32[]{:S(2)}) copy-start(bf16[32,96,3,128]{3,1,2,0:T(8,128)(2,1)S(1)} %all-to-all-done.1) | copy-start | bytes 7077892
  95.8 6.7 %copy-start.12 = (s32[1,2,24]{2,1,0:T(2,128)S(1)}, s32[1,2,24]{2,1,0:T(2,128)}, u32[]{:S(2)}) copy-start(s32[1,2,24]{2,1,0:T(2,128)} %param.19) | copy-start | bytes 580
  95.8 162.6 %all-to-all-start.2 = ((bf16[32,96,3,128]{3,1,2,0:T(8,128)(2,1)}), bf16[32,96,3,128]{3,1,2,0:T(8,128)(2,1)}, u32[]{:S(2)}, u32[]{:S(2)}) async-start(bf16[32,96,3,128]{3,1,2,0:T(8,128)(2,1)} %bitcast.131), calls=%async_computation.2 | async-start | bytes 4718592 | tf_op jit(solution)/shard_map/all_to_all | solution.py:127
  102.7 172.0 %copy-start.8 = (bf16[1,96,3072]{2,1,0:T(8,128)(2,1)S(1)}, bf16[1,96,3072]{2,1,0:T(8,128)(2,1)}, u32[]{:S(2)}) copy-start(bf16[1,96,3072]{2,1,0:T(8,128)(2,1)} %param.17) | copy-start | bytes 1769476
  102.8 155.6 %collective-permute-start.2 = (bf16[96,24,128]{2,1,0:T(8,128)(2,1)S(1)}, bf16[96,24,128]{2,1,0:T(8,128)(2,1)S(1)}, u32[]{:S(2)}, u32[]{:S(2)}) collective-permute-start(bf16[96,24,128]{2,1,0:T(8,128)(2,1)S(1)} %fusion.35), channel_id=1, source_target_pairs={{0,4},{4,0},{1,5},{5,1},{2,6},{6,2},{3,7},{7,3},{8,12},{12,8},{9,1... | collective-permute-start | bytes 1769480 | tf_op jit(solution)/shard_map/ppermute | solution.py:22
  260.2 18.0 %copy-start.11 = (s32[8]{0:T(128)S(1)}, s32[8]{0:T(128)}, u32[]{:S(2)}) copy-start(s32[8]{0:T(128)} %param.21) | copy-start | bytes 100
  260.2 84.0 %all-to-all-start.6 = ((bf16[32,96,3,128]{3,1,2,0:T(8,128)(2,1)}), bf16[32,96,3,128]{3,1,2,0:T(8,128)(2,1)}, u32[]{:S(2)}, u32[]{:S(2)}) async-start(bf16[32,96,3,128]{3,1,2,0:T(8,128)(2,1)} %bitcast.32), calls=%async_computation.6 | async-start | bytes 4718592 | tf_op jit(solution)/shard_map/all_to_all | solution.py:130
  274.6 63.4 %copy-start.4 = (bf16[32,24,3,128]{3,1,2,0:T(8,128)(2,1)S(1)}, bf16[32,24,3,128]{3,1,2,0:T(8,128)(2,1)}, u32[]{:S(2)}) copy-start(bf16[32,24,3,128]{3,1,2,0:T(8,128)(2,1)} %copy-done.3) | copy-start | bytes 1769476
  274.6 64.3 %copy-start.6 = (bf16[32,24,3,128]{3,1,2,0:T(8,128)(2,1)S(1)}, bf16[32,24,3,128]{3,1,2,0:T(8,128)(2,1)}, u32[]{:S(2)}) copy-start(bf16[32,24,3,128]{3,1,2,0:T(8,128)(2,1)} %copy-done.5) | copy-start | bytes 1769476
  274.6 52.0 %collective-permute-start.1 = (bf16[2,24]{1,0:T(2,128)(2,1)S(1)}, bf16[2,24]{1,0:T(2,128)(2,1)S(1)}, u32[]{:S(2)}, u32[]{:S(2)}) collective-permute-start(bf16[2,24]{1,0:T(2,128)(2,1)S(1)} %get-tuple-element.196), channel_id=1, source_target_pairs={{0,4},{4,0},{1,5},{5,1},{2,6},{6,2},{3,7},{7,3},{8,12},{12,8},{9,1... | collective-permute-start | bytes 296 | tf_op jit(solution)/shard_map/ppermute | solution.py:22
  275.2 62.7 %collective-permute-start = (bf16[96,24,128]{2,1,0:T(8,128)(2,1)S(1)}, bf16[96,24,128]{2,1,0:T(8,128)(2,1)S(1)}, u32[]{:S(2)}, u32[]{:S(2)}) collective-permute-start(bf16[96,24,128]{2,1,0:T(8,128)(2,1)S(1)} %fusion.37), channel_id=1, source_target_pairs={{0,4},{4,0},{1,5},{5,1},{2,6},{6,2},{3,7},{7,3},{8,12},{12,8},{9,1... | collective-permute-start | bytes 1769480 | tf_op jit(solution)/shard_map/ppermute | solution.py:22
  346.0 70.6 %all-to-all-start.5 = ((bf16[32,96,3,128]{3,1,2,0:T(8,128)(2,1)}), bf16[32,96,3,128]{3,1,2,0:T(8,128)(2,1)}, u32[]{:S(2)}, u32[]{:S(2)}) async-start(bf16[32,96,3,128]{3,1,2,0:T(8,128)(2,1)} %bitcast.130), calls=%async_computation.5 | async-start | bytes 4718592 | tf_op jit(solution)/shard_map/all_to_all | solution.py:129
  389.7 2.7 copy-start.10
  416.6 58.6 %all-to-all-start.3 = ((bf16[32,24,3,128]{3,1,2,0:T(8,128)(2,1)}), bf16[32,24,3,128]{3,1,2,0:T(8,128)(2,1)S(1)}, u32[]{:S(2)}, u32[]{:S(2)}) async-start(bf16[32,24,3,128]{3,1,2,0:T(8,128)(2,1)} %copy.67), calls=%async_computation.3 | async-start | bytes 1179648 | tf_op jit(solution)/shard_map/all_to_all | solution.py:155
  474.3 28.4 %copy-start.1 = (f32[2,24]{1,0:T(2,128)S(1)}, f32[2,24]{1,0:T(2,128)}, u32[]{:S(2)}) copy-start(f32[2,24]{1,0:T(2,128)} %param.20) | copy-start | bytes 580
  475.2 25.9 %all-to-all-start.7 = ((bf16[32,24,3,128]{3,1,2,0:T(8,128)(2,1)}), bf16[32,24,3,128]{3,1,2,0:T(8,128)(2,1)S(1)}, u32[]{:S(2)}, u32[]{:S(2)}) async-start(bf16[32,24,3,128]{3,1,2,0:T(8,128)(2,1)} %copy.75), calls=%async_computation.7 | async-start | bytes 1179648 | tf_op jit(solution)/shard_map/all_to_all | solution.py:162
where the time goes:
time: 504 us; the launch traced here: 503 us
  waiting for transfers between devices  236 us (47%)
  starting transfers between devices  148 us (29%)
  local copies, waits for them, and re-layouts  50.7 us (10%)
  matrix products  34.8 us (7%)
  other arithmetic  18.1 us (4%)
  loops' own time  13.4 us (3%)
    ppermute x3, waiting for transfers between devices, swapped(): return lax.ppermute(block, axis, route)  149 us
    ppermute x3, starting transfers between devices, swapped(): return lax.ppermute(block, axis, route)  66.9 us
    all_to_all x1, waiting for transfers between devices, per_device(): lax.all_to_all(mine_keys, 'seq', split_axis=0, concat_axis=1, tiled=True)  24.8 us
    all_to_all x1, waiting for transfers between devices, per_device(): lax.all_to_all(pair_keys, 'seq', split_axis=0, concat_axis=1, tiled=True)  23.5 us
    dot_general x6, matrix products, one_block(): jnp.dot(head_queries, head_keys.T, preferred_element_type=jnp.float32)  17.4 us
    dot_general x6, matrix products, one_block(): jnp.dot(weights, head_values, preferred_element_type=jnp.float32)  17.3 us
    all_to_all x1, starting transfers between devices, per_device(): lax.all_to_all(pair_values, 'seq', split_axis=0, concat_axis=1, tiled=True)  14.4 us
    all_to_all x1, starting transfers between devices, per_device(): lax.all_to_all(pair_queries, 'seq', split_axis=0, concat_axis=1, tiled=True)  14.2 us
  transfers between devices with their start and end apart: 11, of which 8 were waited for; matrix products, arithmetic and copies ran while one was open for 18% of the time, Pallas kernels for 0%

commit v1 on v0

v1 whole, which is shorter than its diff:
```python
import functools

import jax
import jax.numpy as jnp
import numpy as np
from jax import lax
from jax.experimental import pallas as pl
from jax.experimental.pallas import tpu as pltpu
from jax.sharding import PartitionSpec as P

HEADS = 24
HD = 128
TOP = 448.0
LOG2E = 1.4426950408889634

NY, NH, NX, NZ = 4, 2, 4, 4
SEATS = NY * NX
HALF = SEATS // 2
PER = HEADS // HALF
BOTH = ("seq", "tower")


def z_route(pick):
    pairs = []
    around = NH * NZ
    for y in range(NY):
        for x in range(NX):
            for z in range(around):
                for core in range(2):

                    def device(at):
                        return (y * NH * NX + (at // NZ) * NX + x) * (2 * NZ) + (at % NZ) * 2 + core

                    pairs.append((device(z), device((z + pick(y * NX + x)) % around)))
    return pairs


def move(block, pick):
    return lax.ppermute(block, BOTH, z_route(pick))


def spread(block):
    groups = [[y * NH * NX + h * NX + x for y in range(NY) for x in range(NX)] for h in range(NH)]
    return lax.all_to_all(block, "seq", 0, 0, axis_index_groups=groups, tiled=True)


def attend_body(slope_ref, base_ref, q_ref, first_ref, second_ref, out_ref, tile_ref, score_ref, *, chunk, run, runs):
    step = pl.program_id(0)
    slope = slope_ref[chunk]

    @pl.when(step == 0)
    def _():
        rows = lax.broadcasted_iota(jnp.int32, (run, run), 0)
        cols = lax.broadcasted_iota(jnp.int32, (run, run), 1)
        tile_ref[...] = (rows - cols).astype(jnp.float32) * slope

    queries = q_ref[...]
    scale = HD ** (-0.5) * LOG2E
    peak = None
    for half, ref in enumerate((first_ref, second_ref)):
        for j in range(runs):
            scores = lax.dot_general(
                queries, ref[j * run : (j + 1) * run, :HD], (((1,), (1,)), ((), ())),
                preferred_element_type=jnp.float32,
            )
            base = ((step - j) * (2 * run) + base_ref[half]).astype(jnp.float32) * slope
            scores = scores * scale - jnp.abs(tile_ref[...] + base)
            at = (half * runs + j) * run
            score_ref[:, at : at + run] = scores
            for lane in range(0, run, 128):
                part = scores[:, lane : lane + 128]
                peak = part if peak is None else jnp.maximum(peak, part)
    peak = jnp.max(peak, axis=1, keepdims=True)
    total = jnp.zeros((run, 128), jnp.float32)
    out = jnp.zeros((run, HD), jnp.float32)
    for half, ref in enumerate((first_ref, second_ref)):
        for j in range(runs):
            at = (half * runs + j) * run
            weights = jnp.exp2(score_ref[:, at : at + run] - peak)
            for lane in range(0, run, 128):
                total = total + weights[:, lane : lane + 128]
            out = out + jnp.dot(
                weights.astype(jnp.bfloat16), ref[j * run : (j + 1) * run, HD:],
                preferred_element_type=jnp.float32,
            )
    out_ref[...] = (out / jnp.sum(total, axis=1, keepdims=True)).astype(jnp.bfloat16)


def attend(slopes, bases, queries, first, second, chunk):
    rows = queries.shape[0]
    runs = NY
    run = rows // runs
    whole = pl.BlockSpec((rows, 2 * HD), lambda i: (0, 0))
    return pl.pallas_call(
        functools.partial(attend_body, chunk=chunk, run=run, runs=runs),
        grid=(runs,),
        in_specs=[
            pl.BlockSpec(memory_space=pltpu.SMEM),
            pl.BlockSpec(memory_space=pltpu.SMEM),
            pl.BlockSpec((run, HD), lambda i: (i, chunk)),
            whole,
            whole,
        ],
        out_specs=pl.BlockSpec((run, HD), lambda i: (i, 0)),
        out_shape=jax.ShapeDtypeStruct((rows, HD), jnp.bfloat16),
        scratch_shapes=[
            pltpu.VMEM((run, run), jnp.float32),
            pltpu.VMEM((run, 2 * rows), jnp.float32),
        ],
        compiler_params=pltpu.CompilerParams(vmem_limit_bytes=32 * 1024 * 1024),
        cost_estimate=pl.CostEstimate(
            flops=8 * rows * rows * HD, bytes_accessed=12 * rows * HD, transcendentals=2 * rows * rows
        ),
    )(slopes, bases, queries, first, second)


def per_device(q_self, k_self, v_self, q_cross, k_cross, v_cross, scale_exps, cross_slopes, offsets):
    rows = q_self.shape[1]
    seat = lax.axis_index("seq")
    tower = lax.axis_index("tower")
    y, high, x = seat // (NH * NX), (seat // NX) % NH, seat % NX
    place = y * NX + x
    crossing = place >= HALF
    z = high * NZ + tower // 2
    towers = lax.axis_size("tower")
    partner = jnp.bitwise_xor(tower, towers // 2)

    def heads_of(matrix):
        return matrix[0].reshape(rows, HALF, PER, HD)

    bound = jnp.exp2(scale_exps[0].astype(jnp.float32)).astype(jnp.bfloat16) * jnp.bfloat16(TOP)
    bound = bound.reshape(2, 1, HALF, PER, 1)
    kc = jnp.clip(heads_of(k_cross), -bound[0], bound[0])
    vc = jnp.clip(heads_of(v_cross), -bound[1], bound[1])
    ks, vs, qs, qc = heads_of(k_self), heads_of(v_self), heads_of(q_self), heads_of(q_cross)

    def pair(keys, values, chunk):
        both = jnp.stack([keys[:, :, chunk], values[:, :, chunk]], axis=2)
        return both.transpose(1, 0, 2, 3).reshape(HALF, rows, 2 * HD)

    def remote(seat_place):
        return NH * NZ // 2 if seat_place < HALF else 2

    def near(seat_place):
        return 0 if seat_place < HALF else -2

    mine = [pair(ks, vs, c) for c in range(PER)]
    other = [pair(kc, vc, c) for c in range(PER)]
    zs = move(mine[0], lambda p: 4)
    zm = move(other[0], lambda p: 2)
    zp = move(other[0], lambda p: -2)
    first, second = [None] * PER, [None] * PER
    for c in range(1, PER):
        block = spread(jnp.concatenate([mine[c], other[c]], axis=0))
        first[c] = move(block, remote)
        second[c] = move(block, near)
    queries = spread(
        jnp.concatenate([m.transpose(1, 0, 2, 3).reshape(HALF, rows, PER * HD) for m in (qs, qc)], axis=0)
    ).reshape(SEATS * rows, PER * HD)
    first[0] = spread(jnp.concatenate([zs, zm], axis=0))
    second[0] = spread(jnp.concatenate([mine[0], zp], axis=0))

    modality = tower // (towers // 2)
    head = jnp.maximum(place - HALF, 0) * PER
    slopes = lax.dynamic_slice(cross_slopes, (modality, head), (1, PER))[0]
    slopes = jnp.where(crossing, slopes * (LOG2E / (SEATS * NH * rows)), 0.0)
    shift = offsets[tower] - offsets[partner]
    run = NX * rows
    bases = jnp.stack(
        [(high - ((z + step) % (NH * NZ)) // NZ) * run + shift for step in (-2, 2)]
    ).astype(jnp.int32)
    outs = []
    for c in range(PER):
        out = attend(
            slopes, bases, queries,
            first[c].reshape(SEATS * rows, 2 * HD), second[c].reshape(SEATS * rows, 2 * HD), c,
        )
        outs.append(spread(out.reshape(SEATS, rows, HD)))
    full = jnp.stack(outs, axis=1).reshape(2, HALF, PER, rows, HD)
    full = full.transpose(0, 3, 1, 2, 4).reshape(2, 1, rows, HEADS * HD)
    return full[0], full[1]


def solution(mesh):
    split = P("tower", "seq", None)
    return jax.shard_map(
        per_device,
        mesh=mesh,
        in_specs=(split,) * 6 + (P("tower", None, None), P(), P()),
        out_specs=(split, split),
        check_vma=False,
    )
```

time: 504 us -> 237 us (0.47)
  the two profiles are of different devices: /device:TPU:2 before, /device:TPU:32 now
where the time goes in v1:
time: 237 us; the launch traced here: 235 us
  starting transfers between devices  87.9 us (37%)
  waiting for transfers between devices  58.1 us (25%)
  Pallas kernels  33.6 us (14%)
  local copies, waits for them, and re-layouts  22.1 us (9%)
  blocking collectives  16.4 us (7%)
  other arithmetic  14.7 us (6%)
    all_to_all x7, starting transfers between devices, spread(): lax.all_to_all(block, 'seq', 0, 0, axis_index_groups=groups, tiled=True)  60.2 us
    ppermute x7, waiting for transfers between devices, move(): return lax.ppermute(block, BOTH, z_route(pick))  41.8 us
    pallas_call x3, Pallas kernels, attend(): pl.pallas_call(functools.partial(attend_body, chunk=chunk, run=run, runs=...  33.6 us
    ppermute x7, starting transfers between devices, move(): return lax.ppermute(block, BOTH, z_route(pick))  27.7 us
    all_to_all x1, blocking collectives, spread(): lax.all_to_all(block, 'seq', 0, 0, axis_index_groups=groups, tiled=True)  16.4 us
    all_to_all x7, waiting for transfers between devices, spread(): lax.all_to_all(block, 'seq', 0, 0, axis_index_groups=groups, tiled=True)  16.3 us
    another operation x6, local copies, waits for them, and re-layouts, heads_of(): return matrix[0].reshape(rows, HALF, PER, HD)  8.09 us
    transpose x4, other arithmetic, pair(): return both.transpose(1, 0, 2, 3).reshape(HALF, rows, 2 * HD)  6.69 us
  transfers between devices with their start and end apart: 14, of which 5 were waited for; matrix products, arithmetic and copies ran while one was open for 6% of the time, Pallas kernels for 14%

profile of v1, /device:TPU:32, one launch (start us, length us, event | category | flops | bytes accessed | tf_op | source)
XLA Modules:
  0.0 235.1 jit_solution(15213306710624987080)
XLA Ops:
  1.5 1.8 reshape_squeeze.20
  4.2 1.8 reshape_squeeze.21
  11.0 1.8 reshape_squeeze.23
  14.2 1.6 maximum_bitcast_fusion.6
  17.1 2.0 pad_maximum_fusion.4
  19.1 7.1 %all-to-all-start.6 = ((bf16[16,96,256]{2,1,0:T(8,128)(2,1)}), bf16[16,96,256]{2,1,0:T(8,128)(2,1)}, u32[]{:S(2)}, u32[]{:S(2)}) async-start(bf16[16,96,256]{2,1,0:T(8,128)(2,1)} %pad_maximum_fusion.4), calls=%async_computation.6 | async-start | bytes 1572864 | tf_op jit(solution)/shard_map/all_to_all | solution.py:44
  26.2 2.5 %maximum_bitcast_fusion.1 = (bf16[8,96,2,128]{3,2,0,1:T(2,128)(2,1)S(1)}, bf16[8,96,2,128]{3,2,0,1:T(2,128)(2,1)}) fusion(bf16[96,8,1,128]{3,2,1,0:T(2,128)(2,1)S(1)} %get-tuple-element.9, bf16[96,8,1,128]{3,2,1,0:T(2,128)(2,1)S(1)} %get-tuple-element.6, bf16[96,8,1,128]{3,2,1,0:T(2,128)(2,1)S(1)} %get-tuple-element.11, ...), kind=kLoop, calls=%fused_computation.8 | loop fusion | flops 1572864 | bytes 1572864 | tf_op jit(solution)/shard_map/transpose | solution.py:139
  30.1 1.6 maximum_bitcast_fusion.2
  33.0 7.7 %all-to-all-done.6 = bf16[16,96,256]{2,1,0:T(8,128)(2,1)} async-done(((bf16[16,96,256]{2,1,0:T(8,128)(2,1)}), bf16[16,96,256]{2,1,0:T(8,128)(2,1)}, u32[]{:S(2)}, u32[]{:S(2)}) %all-to-all-start.6) | async-done | bytes 786464 | tf_op jit(solution)/shard_map/all_to_all | solution.py:44
  40.8 4.3 %all-to-all-start.4 = ((bf16[16,96,256]{2,1,0:T(8,128)(2,1)}), bf16[16,96,256]{2,1,0:T(8,128)(2,1)}, u32[]{:S(2)}, u32[]{:S(2)}) async-start(bf16[16,96,256]{2,1,0:T(8,128)(2,1)} %pad_maximum_fusion.3), calls=%async_computation.4 | async-start | bytes 1572864 | tf_op jit(solution)/shard_map/all_to_all | solution.py:44
  49.7 8.5 %all-to-all-done.4 = bf16[16,96,256]{2,1,0:T(8,128)(2,1)} async-done(((bf16[16,96,256]{2,1,0:T(8,128)(2,1)}), bf16[16,96,256]{2,1,0:T(8,128)(2,1)}, u32[]{:S(2)}, u32[]{:S(2)}) %all-to-all-start.4) | async-done | bytes 786464 | tf_op jit(solution)/shard_map/all_to_all | solution.py:44
  58.2 3.7 %all-to-all-start = ((bf16[16,96,384]{2,1,0:T(8,128)(2,1)}), bf16[16,96,384]{2,1,0:T(8,128)(2,1)S(1)}, u32[]{:S(2)}, u32[]{:S(2)}) async-start(bf16[16,96,384]{2,1,0:T(8,128)(2,1)} %pad_maximum_fusion), calls=%async_computation | async-start | bytes 2359296 | tf_op jit(solution)/shard_map/all_to_all | solution.py:44
  62.2 5.5 %collective-permute-start.2 = (bf16[8,96,256]{2,1,0:T(8,128)(2,1)S(1)}, bf16[8,96,256]{2,1,0:T(8,128)(2,1)S(1)}, u32[]{:S(2)}, u32[]{:S(2)}) collective-permute-start(bf16[8,96,256]{2,1,0:T(8,128)(2,1)S(1)} %copy.35), channel_id=1, source_target_pairs={{0,36},{1,37},{2,38},{3,39},{4,0},{5,1},{6,2},{7,3},{32,4},{33,5},... | collective-permute-start | bytes 1179656 | tf_op jit(solution)/shard_map/ppermute | solution.py:39
  68.1 12.6 %collective-permute-done.2 = bf16[8,96,256]{2,1,0:T(8,128)(2,1)S(1)} collective-permute-done((bf16[8,96,256]{2,1,0:T(8,128)(2,1)S(1)}, bf16[8,96,256]{2,1,0:T(8,128)(2,1)S(1)}, u32[]{:S(2)}, u32[]{:S(2)}) %collective-permute-start.2) | collective-permute-done | bytes 393248 | tf_op jit(solution)/shard_map/ppermute | solution.py:39
  81.7 6.9 %all-to-all-start.2 = ((bf16[16,96,256]{2,1,0:T(8,128)(2,1)}), bf16[16,96,256]{2,1,0:T(8,128)(2,1)S(1)}, u32[]{:S(2)}, u32[]{:S(2)}) async-start(bf16[16,96,256]{2,1,0:T(8,128)(2,1)} %pad_maximum_fusion.2), calls=%async_computation.2 | async-start | bytes 1572864 | tf_op jit(solution)/shard_map/all_to_all | solution.py:44
  88.6 5.0 %collective-permute-start = (bf16[8,96,256]{2,1,0:T(8,128)(2,1)S(1)}, bf16[8,96,256]{2,1,0:T(8,128)(2,1)S(1)}, u32[]{:S(2)}, u32[]{:S(2)}) collective-permute-start(bf16[8,96,256]{2,1,0:T(8,128)(2,1)S(1)} %copy.34), channel_id=1, source_target_pairs={{0,32},{1,33},{2,34},{3,35},{4,36},{5,37},{6,38},{7,39},{32,0},{33... | collective-permute-start | bytes 1179656 | tf_op jit(solution)/shard_map/ppermute | solution.py:39
  93.5 2.1 collective-permute-start.1
  95.6 8.1 %collective-permute-done = bf16[8,96,256]{2,1,0:T(8,128)(2,1)S(1)} collective-permute-done((bf16[8,96,256]{2,1,0:T(8,128)(2,1)S(1)}, bf16[8,96,256]{2,1,0:T(8,128)(2,1)S(1)}, u32[]{:S(2)}, u32[]{:S(2)}) %collective-permute-start) | collective-permute-done | bytes 393248 | tf_op jit(solution)/shard_map/ppermute | solution.py:39
  103.8 21.0 %collective-permute-done.1 = bf16[8,96,256]{2,1,0:T(8,128)(2,1)S(1)} collective-permute-done((bf16[8,96,256]{2,1,0:T(8,128)(2,1)S(1)}, bf16[8,96,256]{2,1,0:T(8,128)(2,1)S(1)}, u32[]{:S(2)}, u32[]{:S(2)}) %collective-permute-start.1) | collective-permute-done | bytes 393248 | tf_op jit(solution)/shard_map/ppermute | solution.py:39
  125.8 11.1 %all-to-all-start.1 = ((bf16[16,96,256]{2,1,0:T(8,128)(2,1)}), bf16[16,96,256]{2,1,0:T(8,128)(2,1)S(1)}, u32[]{:S(2)}, u32[]{:S(2)}) async-start(bf16[16,96,256]{2,1,0:T(8,128)(2,1)} %pad_maximum_fusion.1), calls=%async_computation.1 | async-start | bytes 1572864 | tf_op jit(solution)/shard_map/all_to_all | solution.py:44
  136.9 1.8 collective-permute-start.4
  138.7 4.0 %collective-permute-start.3 = (bf16[16,96,256]{2,1,0:T(8,128)(2,1)}, bf16[16,96,256]{2,1,0:T(8,128)(2,1)}, u32[]{:S(2)}, u32[]{:S(2)}) collective-permute-start(bf16[16,96,256]{2,1,0:T(8,128)(2,1)} %all-to-all-done.4), channel_id=1, source_target_pairs={{0,32},{1,33},{2,34},{3,35},{4,36},{5,37},{6,38},{7,39},{32,0},{33... | collective-permute-start | bytes 2359304 | tf_op jit(solution)/shard_map/ppermute | solution.py:39
  144.6 7.4 %collective-permute-start.6 = (bf16[16,96,256]{2,1,0:T(8,128)(2,1)}, bf16[16,96,256]{2,1,0:T(8,128)(2,1)}, u32[]{:S(2)}, u32[]{:S(2)}) collective-permute-start(bf16[16,96,256]{2,1,0:T(8,128)(2,1)} %all-to-all-done.6), channel_id=1, source_target_pairs={{0,0},{1,1},{2,2},{3,3},{4,4},{5,5},{6,6},{7,7},{32,32},{33,33},{3... | collective-permute-start | bytes 2359304 | tf_op jit(solution)/shard_map/ppermute | solution.py:39
  152.0 2.0 collective-permute-start.5
  154.1 10.9 %shard_map.104 = bf16[1536,128]{1,0:T(8,128)(2,1)} custom-call(f32[3]{0:T(128)S(1)} %fusion.slope_ref, s32[2]{0:T(128)S(1)} %pad_add_fusion.base_ref, bf16[1536,384]{1,0:T(8,128)(2,1)S(1)} %bitcast.50, bf16[1536,256]{1,0:T(8,128)(2,1)S(1)} %bitcast.54, bf16[1536,256]{1,0:T(8,128)(2,1)S(1)} %bitcast.53), custom_call_target="tpu_custom_call" | custom-call | flops 2415919104 | bytes 2359296 | tf_op jit(solution)/shard_map/pallas_call | solution.py:94
  165.0 5.7 %all-to-all-start.3 = ((bf16[16,96,128]{2,1,0:T(8,128)(2,1)}), bf16[16,96,128]{2,1,0:T(8,128)(2,1)S(1)}, u32[]{:S(2)}, u32[]{:S(2)}) async-start(bf16[16,96,128]{2,1,0:T(8,128)(2,1)} %bitcast.11), calls=%async_computation.3 | async-start | bytes 786432 | tf_op jit(solution)/shard_map/all_to_all | solution.py:44
  170.7 11.6 %shard_map.105 = bf16[1536,128]{1,0:T(8,128)(2,1)} custom-call(f32[3]{0:T(128)S(1)} %fusion.slope_ref, s32[2]{0:T(128)S(1)} %pad_add_fusion.base_ref, bf16[1536,384]{1,0:T(8,128)(2,1)S(1)} %bitcast.51, bf16[1536,256]{1,0:T(8,128)(2,1)} %bitcast.15.first_ref, bf16[1536,256]{1,0:T(8,128)(2,1)S(1)} %bitcast.56), custom_call_target="tpu_custom_call" | custom-call | flops 2415919104 | bytes 2359296 | tf_op jit(solution)/shard_map/pallas_call | solution.py:94
  182.3 21.4 %all-to-all-start.5 = ((bf16[16,96,128]{2,1,0:T(8,128)(2,1)}), bf16[16,96,128]{2,1,0:T(8,128)(2,1)S(1)}, u32[]{:S(2)}, u32[]{:S(2)}) async-start(bf16[16,96,128]{2,1,0:T(8,128)(2,1)} %bitcast.17), calls=%async_computation.5 | async-start | bytes 786432 | tf_op jit(solution)/shard_map/all_to_all | solution.py:44
  203.8 11.1 %shard_map.106 = bf16[1536,128]{1,0:T(8,128)(2,1)S(1)} custom-call(f32[3]{0:T(128)S(1)} %fusion.slope_ref, s32[2]{0:T(128)S(1)} %pad_add_fusion.base_ref, bf16[1536,384]{1,0:T(8,128)(2,1)S(1)} %bitcast.52, bf16[1536,256]{1,0:T(8,128)(2,1)} %bitcast.21.first_ref, bf16[1536,256]{1,0:T(8,128)(2,1)} %bitcast.22.second_ref), custom_call_target="tpu_custom_call" | custom-call | flops 2415919104 | bytes 2359296 | tf_op jit(solution)/shard_map/pallas_call | solution.py:94
  214.9 16.4 %all_to_all.40 = bf16[16,96,128]{2,1,0:T(8,128)(2,1)S(1)} all-to-all(bf16[16,96,128]{2,1,0:T(8,128)(2,1)S(1)} %bitcast.55), channel_id=1, replica_groups={{0,8,16,24,64,72,80,88,128,136,144,152,192,200,208,216},{32,40,48,56,96..., dimensions={0} | all-to-all | bytes 786432 | tf_op jit(solution)/shard_map/all_to_all | solution.py:44
  232.1 1.2 squeeze.5
  233.9 1.2 squeeze.4
  (62 shorter events, 21.0 us)
Async XLA Ops:
  6.9 2.0 copy-start
  19.1 21.6 %all-to-all-start.6 = ((bf16[16,96,256]{2,1,0:T(8,128)(2,1)}), bf16[16,96,256]{2,1,0:T(8,128)(2,1)}, u32[]{:S(2)}, u32[]{:S(2)}) async-start(bf16[16,96,256]{2,1,0:T(8,128)(2,1)} %pad_maximum_fusion.4), calls=%async_computation.6 | async-start | bytes 1572864 | tf_op jit(solution)/shard_map/all_to_all | solution.py:44
  33.0 12.0 %copy-start.1 = (bf16[1,96,3072]{2,1,0:T(8,128)(2,1)S(1)}, bf16[1,96,3072]{2,1,0:T(8,128)(2,1)}, u32[]{:S(2)}) copy-start(bf16[1,96,3072]{2,1,0:T(8,128)(2,1)} %param.9) | copy-start | bytes 1769476
  40.8 17.4 %all-to-all-start.4 = ((bf16[16,96,256]{2,1,0:T(8,128)(2,1)}), bf16[16,96,256]{2,1,0:T(8,128)(2,1)}, u32[]{:S(2)}, u32[]{:S(2)}) async-start(bf16[16,96,256]{2,1,0:T(8,128)(2,1)} %pad_maximum_fusion.3), calls=%async_computation.4 | async-start | bytes 1572864 | tf_op jit(solution)/shard_map/all_to_all | solution.py:44
  46.0 1.1 copy-start.2
  58.2 23.5 %all-to-all-start = ((bf16[16,96,384]{2,1,0:T(8,128)(2,1)}), bf16[16,96,384]{2,1,0:T(8,128)(2,1)S(1)}, u32[]{:S(2)}, u32[]{:S(2)}) async-start(bf16[16,96,384]{2,1,0:T(8,128)(2,1)} %pad_maximum_fusion), calls=%async_computation | async-start | bytes 2359296 | tf_op jit(solution)/shard_map/all_to_all | solution.py:44
  62.2 18.4 %collective-permute-start.2 = (bf16[8,96,256]{2,1,0:T(8,128)(2,1)S(1)}, bf16[8,96,256]{2,1,0:T(8,128)(2,1)S(1)}, u32[]{:S(2)}, u32[]{:S(2)}) collective-permute-start(bf16[8,96,256]{2,1,0:T(8,128)(2,1)S(1)} %copy.35), channel_id=1, source_target_pairs={{0,36},{1,37},{2,38},{3,39},{4,0},{5,1},{6,2},{7,3},{32,4},{33,5},... | collective-permute-start | bytes 1179656 | tf_op jit(solution)/shard_map/ppermute | solution.py:39
  81.7 44.1 %all-to-all-start.2 = ((bf16[16,96,256]{2,1,0:T(8,128)(2,1)}), bf16[16,96,256]{2,1,0:T(8,128)(2,1)S(1)}, u32[]{:S(2)}, u32[]{:S(2)}) async-start(bf16[16,96,256]{2,1,0:T(8,128)(2,1)} %pad_maximum_fusion.2), calls=%async_computation.2 | async-start | bytes 1572864 | tf_op jit(solution)/shard_map/all_to_all | solution.py:44
  88.6 15.2 %collective-permute-start = (bf16[8,96,256]{2,1,0:T(8,128)(2,1)S(1)}, bf16[8,96,256]{2,1,0:T(8,128)(2,1)S(1)}, u32[]{:S(2)}, u32[]{:S(2)}) collective-permute-start(bf16[8,96,256]{2,1,0:T(8,128)(2,1)S(1)} %copy.34), channel_id=1, source_target_pairs={{0,32},{1,33},{2,34},{3,35},{4,36},{5,37},{6,38},{7,39},{32,0},{33... | collective-permute-start | bytes 1179656 | tf_op jit(solution)/shard_map/ppermute | solution.py:39
  93.5 31.3 %collective-permute-start.1 = (bf16[8,96,256]{2,1,0:T(8,128)(2,1)S(1)}, bf16[8,96,256]{2,1,0:T(8,128)(2,1)S(1)}, u32[]{:S(2)}, u32[]{:S(2)}) collective-permute-start(bf16[8,96,256]{2,1,0:T(8,128)(2,1)S(1)} %copy.35), channel_id=1, source_target_pairs={{0,4},{1,5},{2,6},{3,7},{4,32},{5,33},{6,34},{7,35},{32,36},{33,37... | collective-permute-start | bytes 1179656 | tf_op jit(solution)/shard_map/ppermute | solution.py:39
  125.8 16.9 %copy-start.3 = (s32[8]{0:T(128)S(1)}, s32[8]{0:T(128)}, u32[]{:S(2)}) copy-start(s32[8]{0:T(128)} %param.17) | copy-start | bytes 100
  125.8 28.2 %copy-start.4 = (f32[2,24]{1,0:T(2,128)S(1)}, f32[2,24]{1,0:T(2,128)}, u32[]{:S(2)}) copy-start(f32[2,24]{1,0:T(2,128)} %param.16) | copy-start | bytes 580
  125.8 28.3 %all-to-all-start.1 = ((bf16[16,96,256]{2,1,0:T(8,128)(2,1)}), bf16[16,96,256]{2,1,0:T(8,128)(2,1)S(1)}, u32[]{:S(2)}, u32[]{:S(2)}) async-start(bf16[16,96,256]{2,1,0:T(8,128)(2,1)} %pad_maximum_fusion.1), calls=%async_computation.1 | async-start | bytes 1572864 | tf_op jit(solution)/shard_map/all_to_all | solution.py:44
  136.9 33.8 %collective-permute-start.4 = (bf16[16,96,256]{2,1,0:T(8,128)(2,1)}, bf16[16,96,256]{2,1,0:T(8,128)(2,1)S(1)}, u32[]{:S(2)}, u32[]{:S(2)}) collective-permute-start(bf16[16,96,256]{2,1,0:T(8,128)(2,1)} %all-to-all-done.4), channel_id=1, source_target_pairs={{0,0},{1,1},{2,2},{3,3},{4,4},{5,5},{6,6},{7,7},{32,32},{33,33},{3... | collective-permute-start | bytes 2359304 | tf_op jit(solution)/shard_map/ppermute | solution.py:39
  138.7 32.1 %collective-permute-start.3 = (bf16[16,96,256]{2,1,0:T(8,128)(2,1)}, bf16[16,96,256]{2,1,0:T(8,128)(2,1)}, u32[]{:S(2)}, u32[]{:S(2)}) collective-permute-start(bf16[16,96,256]{2,1,0:T(8,128)(2,1)} %all-to-all-done.4), channel_id=1, source_target_pairs={{0,32},{1,33},{2,34},{3,35},{4,36},{5,37},{6,38},{7,39},{32,0},{33... | collective-permute-start | bytes 2359304 | tf_op jit(solution)/shard_map/ppermute | solution.py:39
  144.6 59.1 %collective-permute-start.6 = (bf16[16,96,256]{2,1,0:T(8,128)(2,1)}, bf16[16,96,256]{2,1,0:T(8,128)(2,1)}, u32[]{:S(2)}, u32[]{:S(2)}) collective-permute-start(bf16[16,96,256]{2,1,0:T(8,128)(2,1)} %all-to-all-done.6), channel_id=1, source_target_pairs={{0,0},{1,1},{2,2},{3,3},{4,4},{5,5},{6,6},{7,7},{32,32},{33,33},{3... | collective-permute-start | bytes 2359304 | tf_op jit(solution)/shard_map/ppermute | solution.py:39
  152.0 51.7 %collective-permute-start.5 = (bf16[16,96,256]{2,1,0:T(8,128)(2,1)}, bf16[16,96,256]{2,1,0:T(8,128)(2,1)}, u32[]{:S(2)}, u32[]{:S(2)}) collective-permute-start(bf16[16,96,256]{2,1,0:T(8,128)(2,1)} %all-to-all-done.6), channel_id=1, source_target_pairs={{0,32},{1,33},{2,34},{3,35},{4,36},{5,37},{6,38},{7,39},{32,0},{33... | collective-permute-start | bytes 2359304 | tf_op jit(solution)/shard_map/ppermute | solution.py:39
  165.0 17.3 %all-to-all-start.3 = ((bf16[16,96,128]{2,1,0:T(8,128)(2,1)}), bf16[16,96,128]{2,1,0:T(8,128)(2,1)S(1)}, u32[]{:S(2)}, u32[]{:S(2)}) async-start(bf16[16,96,128]{2,1,0:T(8,128)(2,1)} %bitcast.11), calls=%async_computation.3 | async-start | bytes 786432 | tf_op jit(solution)/shard_map/all_to_all | solution.py:44
  182.3 32.6 %all-to-all-start.5 = ((bf16[16,96,128]{2,1,0:T(8,128)(2,1)}), bf16[16,96,128]{2,1,0:T(8,128)(2,1)S(1)}, u32[]{:S(2)}, u32[]{:S(2)}) async-start(bf16[16,96,128]{2,1,0:T(8,128)(2,1)} %bitcast.17), calls=%async_computation.5 | async-start | bytes 786432 | tf_op jit(solution)/shard_map/all_to_all | solution.py:44

commit v2 on v1

--- a/solution.py
+++ b/solution.py
@@ -18,6 +18,8 @@
 HALF = SEATS // 2
 PER = HEADS // HALF
 BOTH = ("seq", "tower")
+VMEM_LIMIT = 32 * 1024 * 1024
+PACK_LIMIT = 60 * 1024 * 1024
 
 
 def z_route(pick):
@@ -86,20 +88,20 @@
     out_ref[...] = (out / jnp.sum(total, axis=1, keepdims=True)).astype(jnp.bfloat16)
 
 
-def attend(slopes, bases, queries, first, second, chunk):
+def attend(slopes, bases, queries, first, second, chunk, cols=(0, 0)):
     rows = queries.shape[0]
     runs = NY
     run = rows // runs
-    whole = pl.BlockSpec((rows, 2 * HD), lambda i: (0, 0))
+    at = queries.shape[1] // HD - PER + chunk
     return pl.pallas_call(
         functools.partial(attend_body, chunk=chunk, run=run, runs=runs),
         grid=(runs,),
         in_specs=[
             pl.BlockSpec(memory_space=pltpu.SMEM),
             pl.BlockSpec(memory_space=pltpu.SMEM),
-            pl.BlockSpec((run, HD), lambda i: (i, chunk)),
-            whole,
-            whole,
+            pl.BlockSpec((run, HD), lambda i: (i, at)),
+            pl.BlockSpec((rows, 2 * HD), lambda i: (0, cols[0])),
+            pl.BlockSpec((rows, 2 * HD), lambda i: (0, cols[1])),
         ],
         out_specs=pl.BlockSpec((run, HD), lambda i: (i, 0)),
         out_shape=jax.ShapeDtypeStruct((rows, HD), jnp.bfloat16),
@@ -107,11 +109,100 @@
             pltpu.VMEM((run, run), jnp.float32),
             pltpu.VMEM((run, 2 * rows), jnp.float32),
         ],
-        compiler_params=pltpu.CompilerParams(vmem_limit_bytes=32 * 1024 * 1024),
+        compiler_params=pltpu.CompilerParams(vmem_limit_bytes=VMEM_LIMIT),
         cost_estimate=pl.CostEstimate(
             flops=8 * rows * rows * HD, bytes_accessed=12 * rows * HD, transcendentals=2 * rows * rows
         ),
     )(slopes, bases, queries, first, second)
+
+
+def pack_body(bound_ref, *refs, chunk, count):
+    out_refs = refs[4 * count :]
+    mine = out_refs[0]
+    other = out_refs[1] if len(out_refs) > 1 else out_refs[0].at[HALF:]
+    for c in range(count):
+        ks_ref, vs_ref, kc_ref, vc_ref = refs[4 * c : 4 * c + 4]
+        for j in range(HALF):
+            cols = slice(j * HD, (j + 1) * HD)
+            for kind, ref in enumerate((ks_ref, vs_ref)):
+                mine[j, :, (2 * c + kind) * HD : (2 * c + kind + 1) * HD] = ref[:, cols]
+            for kind, ref in enumerate((kc_ref, vc_ref)):
+                top = bound_ref[kind, (chunk + c) * HALF + j]
+                block = jnp.clip(ref[:, cols].astype(jnp.float32), -top, top)
+                other[j, :, (2 * c + kind) * HD : (2 * c + kind + 1) * HD] = block.astype(jnp.bfloat16)
+
+
+def pack(bounds, arrays, chunk, count, apart):
+    rows = arrays[0].shape[0]
+    outputs, seats = (2, HALF) if apart else (1, SEATS)
+    shape = (seats, rows, count * 2 * HD)
+
+    def source(c):
+        return pl.BlockSpec((rows, HALF * HD), lambda i: (0, c))
+
+    return pl.pallas_call(
+        functools.partial(pack_body, chunk=chunk, count=count),
+        grid=(1,),
+        in_specs=[pl.BlockSpec(memory_space=pltpu.SMEM)] + [source(chunk + c) for c in range(count) for _ in range(4)],
+        out_specs=[pl.BlockSpec(shape, lambda i: (0, 0, 0))] * outputs,
+        out_shape=[jax.ShapeDtypeStruct(shape, jnp.bfloat16)] * outputs,
+        compiler_params=pltpu.CompilerParams(vmem_limit_bytes=PACK_LIMIT),
+    )(bounds, *(arrays * count))
+
+
+def join_body(zs_ref, zm_ref, mine_ref, zp_ref, qs_ref, qc_ref, out_ref):
+    for j in range(HALF):
+        out_ref[j, :, : 2 * HD] = zs_ref[j]
+        out_ref[HALF + j, :, : 2 * HD] = zm_ref[j]
+        out_ref[j, :, 2 * HD : 4 * HD] = mine_ref[j]
+        out_ref[HALF + j, :, 2 * HD : 4 * HD] = zp_ref[j]
+        for c in range(PER):
+            cols = slice((c * HALF + j) * HD, (c * HALF + j + 1) * HD)
+            out_ref[j, :, (4 + c) * HD : (5 + c) * HD] = qs_ref[:, cols]
+            out_ref[HALF + j, :, (4 + c) * HD : (5 + c) * HD] = qc_ref[:, cols]
+
+
+def join(*arrays):
+    rows = arrays[0].shape[1]
+    shape = (SEATS, rows, (4 + PER) * HD)
+
+    def whole(array_shape):
+        return pl.BlockSpec(array_shape, lambda i: (0,) * len(array_shape))
+
+    return pl.pallas_call(
+        join_body,
+        grid=(1,),
+        in_specs=[whole(a.shape) for a in arrays],
+        out_specs=whole(shape),
+        out_shape=jax.ShapeDtypeStruct(shape, jnp.bfloat16),
+        compiler_params=pltpu.CompilerParams(vmem_limit_bytes=VMEM_LIMIT),
+    )(*arrays)
+
+
+def unpack_body(*refs):
+    self_ref, cross_ref = refs[PER:]
+    for chunk in range(PER):
+        for j in range(HALF):
+            head = chunk * HALF + j
+            cols = slice(head * HD, (head + 1) * HD)
+            self_ref[:, cols] = refs[chunk][j]
+            cross_ref[:, cols] = refs[chunk][HALF + j]
+
+
+def unpack(*chunks):
+    rows = chunks[0].shape[1]
+    vmem = pl.BlockSpec(memory_space=pltpu.VMEM)
+    return pl.pallas_call(
+        unpack_body,
+        in_specs=[vmem] * PER,
+        out_specs=[vmem] * 2,
+        out_shape=[jax.ShapeDtypeStruct((rows, HEADS * HD), jnp.bfloat16)] * 2,
+        compiler_params=pltpu.CompilerParams(vmem_limit_bytes=VMEM_LIMIT),
+    )(*chunks)
+
+
+def after(value, *others):
+    return lax.optimization_barrier((value,) + others)[0]
 
 
 def per_device(q_self, k_self, v_self, q_cross, k_cross, v_cross, scale_exps, cross_slopes, offsets):
@@ -125,60 +216,46 @@
     towers = lax.axis_size("tower")
     partner = jnp.bitwise_xor(tower, towers // 2)
 
-    def heads_of(matrix):
-        return matrix[0].reshape(rows, HALF, PER, HD)
-
-    bound = jnp.exp2(scale_exps[0].astype(jnp.float32)).astype(jnp.bfloat16) * jnp.bfloat16(TOP)
-    bound = bound.reshape(2, 1, HALF, PER, 1)
-    kc = jnp.clip(heads_of(k_cross), -bound[0], bound[0])
-    vc = jnp.clip(heads_of(v_cross), -bound[1], bound[1])
-    ks, vs, qs, qc = heads_of(k_self), heads_of(v_self), heads_of(q_self), heads_of(q_cross)
-
-    def pair(keys, values, chunk):
-        both = jnp.stack([keys[:, :, chunk], values[:, :, chunk]], axis=2)
-        return both.transpose(1, 0, 2, 3).reshape(HALF, rows, 2 * HD)
-
-    def remote(seat_place):
-        return NH * NZ // 2 if seat_place < HALF else 2
-
-    def near(seat_place):
-        return 0 if seat_place < HALF else -2
-
-    mine = [pair(ks, vs, c) for c in range(PER)]
-    other = [pair(kc, vc, c) for c in range(PER)]
-    zs = move(mine[0], lambda p: 4)
-    zm = move(other[0], lambda p: 2)
-    zp = move(other[0], lambda p: -2)
-    first, second = [None] * PER, [None] * PER
-    for c in range(1, PER):
-        block = spread(jnp.concatenate([mine[c], other[c]], axis=0))
-        first[c] = move(block, remote)
-        second[c] = move(block, near)
-    queries = spread(
-        jnp.concatenate([m.transpose(1, 0, 2, 3).reshape(HALF, rows, PER * HD) for m in (qs, qc)], axis=0)
-    ).reshape(SEATS * rows, PER * HD)
-    first[0] = spread(jnp.concatenate([zs, zm], axis=0))
-    second[0] = spread(jnp.concatenate([mine[0], zp], axis=0))
-
     modality = tower // (towers // 2)
-    head = jnp.maximum(place - HALF, 0) * PER
-    slopes = lax.dynamic_slice(cross_slopes, (modality, head), (1, PER))[0]
+    slopes = cross_slopes.reshape(2, PER, HALF)[modality, :, place % HALF]
     slopes = jnp.where(crossing, slopes * (LOG2E / (SEATS * NH * rows)), 0.0)
     shift = offsets[tower] - offsets[partner]
     run = NX * rows
     bases = jnp.stack(
         [(high - ((z + step) % (NH * NZ)) // NZ) * run + shift for step in (-2, 2)]
     ).astype(jnp.int32)
+
+    bounds = jnp.exp2(scale_exps[0].astype(jnp.float32)).astype(jnp.bfloat16).astype(jnp.float32) * TOP
+
+    def remote(seat_place):
+        return NH * NZ // 2 if seat_place < HALF else 2
+
+    def near(seat_place):
+        return 0 if seat_place < HALF else -2
+
+    arrays = (k_self[0], v_self[0], k_cross[0], v_cross[0])
+    mine, other = pack(bounds, arrays, 0, 1, True)
+    zs = move(mine, lambda p: NH * NZ // 2)
+    zm = move(other, lambda p: 2)
+    zp = move(other, lambda p: -2)
+    block = spread(pack(bounds, arrays, 1, 2, False)[0])
+    zs, zm, zp, block = lax.optimization_barrier((zs, zm, zp, block))
+    blocks = [block[:, :, : 2 * HD], block[:, :, 2 * HD :]]
+    first, second = [move(blocks[0], remote)], [move(blocks[0], near)]
+    joined = spread(join(zs, zm, mine, zp, q_self[0], q_cross[0]))
+    last = blocks[1]
+    first, second = first + [move(last, remote)], second + [move(last, near)]
+    joined = joined.reshape(SEATS * rows, (4 + PER) * HD)
     outs = []
     for c in range(PER):
-        out = attend(
-            slopes, bases, queries,
-            first[c].reshape(SEATS * rows, 2 * HD), second[c].reshape(SEATS * rows, 2 * HD), c,
-        )
+        if c:
+            halves, cols = (a[c - 1].reshape(SEATS * rows, 2 * HD) for a in (first, second)), (0, 0)
+        else:
+            halves, cols = (joined, joined), (0, 1)
+        out = attend(slopes, bases, joined, *halves, c, cols)
         outs.append(spread(out.reshape(SEATS, rows, HD)))
-    full = jnp.stack(outs, axis=1).reshape(2, HALF, PER, rows, HD)
-    full = full.transpose(0, 3, 1, 2, 4).reshape(2, 1, rows, HEADS * HD)
-    return full[0], full[1]
+    mine, other = unpack(*outs)
+    return mine[None], other[None]
 
 
 def solution(mesh):

time: 237 us -> 178 us (0.75)
  starting transfers between devices: 87.9 us -> 56.7 us
  local copies, waits for them, and re-layouts: 22.1 us -> 5.82 us
  other arithmetic: 14.7 us -> 1.54 us
  Pallas kernels: 33.6 us -> 41.6 us
  waiting for transfers between devices: 58.1 us -> 54.3 us
    all_to_all x7 -> x4, starting transfers between devices: 60.2 us -> 26.8 us  [spread(): lax.all_to_all(block, 'seq', 0, 0, axis_index_groups=groups, tiled=True)]
    pallas_call x0 -> x4, Pallas kernels: none -> 8.41 us  [the longest x2 5.21 us: pack(): pl.pallas_call(functools.partial(pack_body, chunk=chunk, count=count), gr...]
    another operation x6 -> x0, local copies, waits for them, and re-layouts: 8.09 us -> none  [heads_of(): return matrix[0].reshape(rows, HALF, PER, HD)]
    transpose x5 -> x0, other arithmetic: 6.82 us -> none  [the longest x4 6.69 us: pair(): return both.transpose(1, 0, 2, 3).reshape(HALF, rows, 2 * HD)]
    concatenate x5 -> x0, other arithmetic: 6.05 us -> none  [the longest x2 2.98 us: per_device(): block = spread(jnp.concatenate([mine[c], other[c]], axis=0))]
    reshape x16 -> x1, local copies, waits for them, and re-layouts: 5.92 us -> 0.08 us  [per_device(): slopes = cross_slopes.reshape(2, PER, HALF)[modality, :, place % HALF]]
    ppermute x7, waiting for transfers between devices: 41.8 us -> 37.9 us  [move(): return lax.ppermute(block, BOTH, z_route(pick))]
    squeeze x2 -> x0, local copies, waits for them, and re-layouts: 2.5 us -> none  [per_device(): return (full[0], full[1])]
  transfers between devices with their start and end apart: 14 -> 11, of which waited for: 5 -> 6; matrix products, arithmetic and copies ran while one was open for 6% -> 2% of each run, Pallas kernels for 14% -> 20%
where the time goes in v2:
time: 178 us; the launch traced here: 177 us
  starting transfers between devices  56.7 us (32%)
  waiting for transfers between devices  54.3 us (31%)
  Pallas kernels  41.6 us (23%)
  blocking collectives  14.8 us (8%)
  local copies, waits for them, and re-layouts  5.82 us (3%)
  between operations  2.08 us (1%)
    ppermute x7, waiting for transfers between devices, move(): return lax.ppermute(block, BOTH, z_route(pick))  37.9 us
    pallas_call x3, Pallas kernels, attend(): pl.pallas_call(functools.partial(attend_body, chunk=chunk, run=run, runs=...  33.2 us
    ppermute x7, starting transfers between devices, move(): return lax.ppermute(block, BOTH, z_route(pick))  29.9 us
    all_to_all x4, starting transfers between devices, spread(): lax.all_to_all(block, 'seq', 0, 0, axis_index_groups=groups, tiled=True)  26.8 us
    all_to_all x4, waiting for transfers between devices, spread(): lax.all_to_all(block, 'seq', 0, 0, axis_index_groups=groups, tiled=True)  16.3 us
    all_to_all x1, blocking collectives, spread(): lax.all_to_all(block, 'seq', 0, 0, axis_index_groups=groups, tiled=True)  14.8 us
    pallas_call x2, Pallas kernels, pack(): pl.pallas_call(functools.partial(pack_body, chunk=chunk, count=count), gr...  5.21 us
  transfers between devices with their start and end apart: 11, of which 6 were waited for; matrix products, arithmetic and copies ran while one was open for 2% of the time, Pallas kernels for 20%

profile of v2, /device:TPU:32, one launch (start us, length us, event | category | flops | bytes accessed | tf_op | source)
XLA Modules:
  0.0 176.9 jit_solution(13793026448040510940)
XLA Ops:
  0.6 1.3 multiply_bitcast_fusion.bound_ref
  1.9 2.9 %shard_map.105 = bf16[16,96,512]{2,1,0:T(8,128)(2,1)} custom-call(f32[2,24]{1,0:T(2,128)} %multiply_bitcast_fusion.bound_ref, bf16[96,3072]{1,0:T(8,128)(2,1)} %bitcast.30, bf16[96,3072]{1,0:T(8,128)(2,1)} %bitcast.33, bf16[96,3072]{1,0:T(8,128)(2,1)} %bitcast.36, bf16[96,3072]{1,0:T(8,128)(2,1)} %bitcast.39, bf16[96,3072]{1,0:T(8,128)(2,1)} %bitcast.31, ...), custom_call_target="tpu_custom_call" | custom-call | tf_op jit(solution)/shard_map/pallas_call | solution.py:143
  4.8 7.1 %all-to-all-start = ((bf16[16,96,512]{2,1,0:T(8,128)(2,1)}), bf16[16,96,512]{2,1,0:T(8,128)(2,1)}, u32[]{:S(2)}, u32[]{:S(2)}) async-start(bf16[16,96,512]{2,1,0:T(8,128)(2,1)} %shard_map.105), calls=%async_computation | async-start | bytes 3145728 | tf_op jit(solution)/shard_map/all_to_all | solution.py:46
  11.9 2.3 %shard_map.104 = (bf16[8,96,256]{2,1,0:T(8,128)(2,1)}, bf16[8,96,256]{2,1,0:T(8,128)(2,1)}) custom-call(f32[2,24]{1,0:T(2,128)} %multiply_bitcast_fusion.bound_ref, bf16[96,3072]{1,0:T(8,128)(2,1)} %bitcast.32, bf16[96,3072]{1,0:T(8,128)(2,1)} %bitcast.35, bf16[96,3072]{1,0:T(8,128)(2,1)} %bitcast.38, bf16[96,3072]{1,0:T(8,128)(2,1)} %bitcast.41), custom_call_target="tpu_custom_call" | custom-call | tf_op jit(solution)/shard_map/pallas_call | solution.py:143
  14.2 6.3 %collective-permute-start = (bf16[8,96,256]{2,1,0:T(8,128)(2,1)}, bf16[8,96,256]{2,1,0:T(8,128)(2,1)S(1)}, u32[]{:S(2)}, u32[]{:S(2)}) collective-permute-start(bf16[8,96,256]{2,1,0:T(8,128)(2,1)} %get-tuple-element.10.mine_ref), channel_id=1, source_target_pairs={{0,32},{1,33},{2,34},{3,35},{4,36},{5,37},{6,38},{7,39},{32,0},{33... | collective-permute-start | bytes 1179656 | tf_op jit(solution)/shard_map/ppermute | solution.py:41
  20.5 0.6 collective-permute-start.2
  21.1 2.4 %collective-permute-start.1 = (bf16[8,96,256]{2,1,0:T(8,128)(2,1)}, bf16[8,96,256]{2,1,0:T(8,128)(2,1)S(1)}, u32[]{:S(2)}, u32[]{:S(2)}) collective-permute-start(bf16[8,96,256]{2,1,0:T(8,128)(2,1)} %get-tuple-element.11), channel_id=1, source_target_pairs={{0,4},{1,5},{2,6},{3,7},{4,32},{5,33},{6,34},{7,35},{32,36},{33,37... | collective-permute-start | bytes 1179656 | tf_op jit(solution)/shard_map/ppermute | solution.py:41
  23.5 17.6 %collective-permute-done.zs_ref = bf16[8,96,256]{2,1,0:T(8,128)(2,1)S(1)} collective-permute-done((bf16[8,96,256]{2,1,0:T(8,128)(2,1)}, bf16[8,96,256]{2,1,0:T(8,128)(2,1)S(1)}, u32[]{:S(2)}, u32[]{:S(2)}) %collective-permute-start) | collective-permute-done | bytes 393248 | tf_op jit(solution)/shard_map/ppermute | solution.py:41
  41.1 7.5 %collective-permute-done.2.zp_ref = bf16[8,96,256]{2,1,0:T(8,128)(2,1)S(1)} collective-permute-done((bf16[8,96,256]{2,1,0:T(8,128)(2,1)}, bf16[8,96,256]{2,1,0:T(8,128)(2,1)S(1)}, u32[]{:S(2)}, u32[]{:S(2)}) %collective-permute-start.2) | collective-permute-done | bytes 393248 | tf_op jit(solution)/shard_map/ppermute | solution.py:41
  48.6 6.2 %collective-permute-done.1.zm_ref = bf16[8,96,256]{2,1,0:T(8,128)(2,1)S(1)} collective-permute-done((bf16[8,96,256]{2,1,0:T(8,128)(2,1)}, bf16[8,96,256]{2,1,0:T(8,128)(2,1)S(1)}, u32[]{:S(2)}, u32[]{:S(2)}) %collective-permute-start.1) | collective-permute-done | bytes 393248 | tf_op jit(solution)/shard_map/ppermute | solution.py:41
  54.8 1.0 copy-done.4
  55.8 1.9 %shard_map.106 = bf16[16,96,896]{2,1,0:T(8,128)(2,1)} custom-call(bf16[8,96,256]{2,1,0:T(8,128)(2,1)S(1)} %collective-permute-done.zs_ref, bf16[8,96,256]{2,1,0:T(8,128)(2,1)S(1)} %collective-permute-done.1.zm_ref, bf16[8,96,256]{2,1,0:T(8,128)(2,1)S(1)} %copy-done.4, bf16[8,96,256]{2,1,0:T(8,128)(2,1)S(1)} %collective-permute-done.2.zp_ref, ...), custom_call_target="tpu_custom_call" | custom-call | tf_op jit(solution)/shard_map/pallas_call | solution.py:172
  57.6 6.9 %all-to-all-start.1 = ((bf16[16,96,896]{2,1,0:T(8,128)(2,1)}), bf16[16,96,896]{2,1,0:T(8,128)(2,1)S(1)}, u32[]{:S(2)}, u32[]{:S(2)}) async-start(bf16[16,96,896]{2,1,0:T(8,128)(2,1)} %shard_map.106), calls=%async_computation.1 | async-start | bytes 5505024 | tf_op jit(solution)/shard_map/all_to_all | solution.py:46
  64.6 2.6 %fusion = (bf16[16,96,256]{2,1,0:T(8,128)(2,1)}, bf16[16,96,256]{2,1,0:T(8,128)(2,1)}) fusion(bf16[16,96,512]{2,1,0:T(8,128)(2,1)} %all-to-all-done), kind=kLoop, calls=%fused_computation.4 | loop fusion | bytes 3145728 | tf_op jit(solution)/shard_map/slice | solution.py:243
  67.2 7.4 %collective-permute-start.6 = (bf16[16,96,256]{2,1,0:T(8,128)(2,1)}, bf16[16,96,256]{2,1,0:T(8,128)(2,1)}, u32[]{:S(2)}, u32[]{:S(2)}) collective-permute-start(bf16[16,96,256]{2,1,0:T(8,128)(2,1)} %get-tuple-element.18), channel_id=1, source_target_pairs={{0,0},{1,1},{2,2},{3,3},{4,4},{5,5},{6,6},{7,7},{32,32},{33,33},{3... | collective-permute-start | bytes 2359304 | tf_op jit(solution)/shard_map/ppermute | solution.py:41
  74.6 5.3 %collective-permute-start.5 = (bf16[16,96,256]{2,1,0:T(8,128)(2,1)}, bf16[16,96,256]{2,1,0:T(8,128)(2,1)}, u32[]{:S(2)}, u32[]{:S(2)}) collective-permute-start(bf16[16,96,256]{2,1,0:T(8,128)(2,1)} %get-tuple-element.18), channel_id=1, source_target_pairs={{0,32},{1,33},{2,34},{3,35},{4,36},{5,37},{6,38},{7,39},{32,0},{33... | collective-permute-start | bytes 2359304 | tf_op jit(solution)/shard_map/ppermute | solution.py:41
  79.9 0.6 fusion.1
  81.8 7.4 %collective-permute-start.4 = (bf16[16,96,256]{2,1,0:T(8,128)(2,1)}, bf16[16,96,256]{2,1,0:T(8,128)(2,1)}, u32[]{:S(2)}, u32[]{:S(2)}) collective-permute-start(bf16[16,96,256]{2,1,0:T(8,128)(2,1)} %get-tuple-element.19), channel_id=1, source_target_pairs={{0,0},{1,1},{2,2},{3,3},{4,4},{5,5},{6,6},{7,7},{32,32},{33,33},{3... | collective-permute-start | bytes 2359304 | tf_op jit(solution)/shard_map/ppermute | solution.py:41
  89.2 0.6 collective-permute-start.3
  90.0 0.2 select_reduce_fusion.slope_ref
  90.2 16.3 %all-to-all-done.1 = bf16[16,96,896]{2,1,0:T(8,128)(2,1)S(1)} async-done(((bf16[16,96,896]{2,1,0:T(8,128)(2,1)}), bf16[16,96,896]{2,1,0:T(8,128)(2,1)S(1)}, u32[]{:S(2)}, u32[]{:S(2)}) %all-to-all-start.1) | async-done | bytes 2752544 | tf_op jit(solution)/shard_map/all_to_all | solution.py:46
  106.5 10.9 %shard_map.107 = bf16[1536,128]{1,0:T(8,128)(2,1)} custom-call(f32[3]{0:T(128)S(1)} %select_reduce_fusion.slope_ref, s32[2]{0:T(128)S(1)} %pad_add_fusion.base_ref, bf16[1536,896]{1,0:T(8,128)(2,1)S(1)} %bitcast.21, bf16[1536,896]{1,0:T(8,128)(2,1)S(1)} %bitcast.22, bf16[1536,896]{1,0:T(8,128)(2,1)S(1)} %bitcast.23), custom_call_target="tpu_custom_call" | custom-call | flops 2415919104 | bytes 2359296 | tf_op jit(solution)/shard_map/pallas_call | solution.py:96
  117.4 4.0 %all-to-all-start.2 = ((bf16[16,96,128]{2,1,0:T(8,128)(2,1)}), bf16[16,96,128]{2,1,0:T(8,128)(2,1)S(1)}, u32[]{:S(2)}, u32[]{:S(2)}) async-start(bf16[16,96,128]{2,1,0:T(8,128)(2,1)} %bitcast.11), calls=%async_computation.2 | async-start | bytes 786432 | tf_op jit(solution)/shard_map/all_to_all | solution.py:46
  121.4 1.6 collective-permute-done.5
  123.1 11.1 %shard_map.109 = bf16[1536,128]{1,0:T(8,128)(2,1)S(1)} custom-call(f32[3]{0:T(128)S(1)} %select_reduce_fusion.slope_ref, s32[2]{0:T(128)S(1)} %pad_add_fusion.base_ref, bf16[1536,896]{1,0:T(8,128)(2,1)S(1)} %bitcast.24, bf16[1536,256]{1,0:T(8,128)(2,1)} %bitcast.15.first_ref, bf16[1536,256]{1,0:T(8,128)(2,1)} %bitcast.16.second_ref), custom_call_target="tpu_custom_call" | custom-call | flops 2415919104 | bytes 2359296 | tf_op jit(solution)/shard_map/pallas_call | solution.py:96
  134.2 0.7 copy-done.2
  135.0 8.9 %all-to-all-start.4 = ((bf16[16,96,128]{2,1,0:T(8,128)(2,1)}), bf16[16,96,128]{2,1,0:T(8,128)(2,1)S(1)}, u32[]{:S(2)}, u32[]{:S(2)}) async-start(bf16[16,96,128]{2,1,0:T(8,128)(2,1)} %bitcast.28), calls=%async_computation.4 | async-start | bytes 786432 | tf_op jit(solution)/shard_map/all_to_all | solution.py:46
  143.9 5.0 %collective-permute-done.3 = bf16[16,96,256]{2,1,0:T(8,128)(2,1)} collective-permute-done((bf16[16,96,256]{2,1,0:T(8,128)(2,1)}, bf16[16,96,256]{2,1,0:T(8,128)(2,1)}, u32[]{:S(2)}, u32[]{:S(2)}) %collective-permute-start.3) | collective-permute-done | bytes 786464 | tf_op jit(solution)/shard_map/ppermute | solution.py:41
  148.8 11.1 %shard_map.108 = bf16[1536,128]{1,0:T(8,128)(2,1)S(1)} custom-call(f32[3]{0:T(128)S(1)} %select_reduce_fusion.slope_ref, s32[2]{0:T(128)S(1)} %pad_add_fusion.base_ref, bf16[1536,896]{1,0:T(8,128)(2,1)S(1)} %bitcast.25, bf16[1536,256]{1,0:T(8,128)(2,1)} %bitcast.12.first_ref, bf16[1536,256]{1,0:T(8,128)(2,1)} %bitcast.13.second_ref), custom_call_target="tpu_custom_call" | custom-call | flops 2415919104 | bytes 2359296 | tf_op jit(solution)/shard_map/pallas_call | solution.py:96
  160.0 0.7 copy-done.3
  160.7 14.8 %all_to_all.25.refs_1_ = bf16[16,96,128]{2,1,0:T(8,128)(2,1)S(1)} all-to-all(bf16[16,96,128]{2,1,0:T(8,128)(2,1)} %bitcast.29), channel_id=1, replica_groups={{0,8,16,24,64,72,80,88,128,136,144,152,192,200,208,216},{32,40,48,56,96..., dimensions={0} | all-to-all | bytes 786432 | tf_op jit(solution)/shard_map/all_to_all | solution.py:46
  175.5 1.3 shard_map.110
  (18 shorter events, 0.2 us)
Async XLA Ops:
  4.8 49.9 %all-to-all-start = ((bf16[16,96,512]{2,1,0:T(8,128)(2,1)}), bf16[16,96,512]{2,1,0:T(8,128)(2,1)}, u32[]{:S(2)}, u32[]{:S(2)}) async-start(bf16[16,96,512]{2,1,0:T(8,128)(2,1)} %shard_map.105), calls=%async_computation | async-start | bytes 3145728 | tf_op jit(solution)/shard_map/all_to_all | solution.py:46
  11.9 42.9 %copy-start = (bf16[1,96,3072]{2,1,0:T(8,128)(2,1)S(1)}, bf16[1,96,3072]{2,1,0:T(8,128)(2,1)}, u32[]{:S(2)}) copy-start(bf16[1,96,3072]{2,1,0:T(8,128)(2,1)} %param.9) | copy-start | bytes 1769476
  11.9 42.8 %copy-start.1 = (bf16[1,96,3072]{2,1,0:T(8,128)(2,1)S(1)}, bf16[1,96,3072]{2,1,0:T(8,128)(2,1)}, u32[]{:S(2)}) copy-start(bf16[1,96,3072]{2,1,0:T(8,128)(2,1)} %param.12) | copy-start | bytes 1769476
  14.2 26.8 %collective-permute-start = (bf16[8,96,256]{2,1,0:T(8,128)(2,1)}, bf16[8,96,256]{2,1,0:T(8,128)(2,1)S(1)}, u32[]{:S(2)}, u32[]{:S(2)}) collective-permute-start(bf16[8,96,256]{2,1,0:T(8,128)(2,1)} %get-tuple-element.10.mine_ref), channel_id=1, source_target_pairs={{0,32},{1,33},{2,34},{3,35},{4,36},{5,37},{6,38},{7,39},{32,0},{33... | collective-permute-start | bytes 1179656 | tf_op jit(solution)/shard_map/ppermute | solution.py:41
  20.5 28.0 %collective-permute-start.2 = (bf16[8,96,256]{2,1,0:T(8,128)(2,1)}, bf16[8,96,256]{2,1,0:T(8,128)(2,1)S(1)}, u32[]{:S(2)}, u32[]{:S(2)}) collective-permute-start(bf16[8,96,256]{2,1,0:T(8,128)(2,1)} %get-tuple-element.11), channel_id=1, source_target_pairs={{0,36},{1,37},{2,38},{3,39},{4,0},{5,1},{6,2},{7,3},{32,4},{33,5},... | collective-permute-start | bytes 1179656 | tf_op jit(solution)/shard_map/ppermute | solution.py:41
  21.1 33.7 %collective-permute-start.1 = (bf16[8,96,256]{2,1,0:T(8,128)(2,1)}, bf16[8,96,256]{2,1,0:T(8,128)(2,1)S(1)}, u32[]{:S(2)}, u32[]{:S(2)}) collective-permute-start(bf16[8,96,256]{2,1,0:T(8,128)(2,1)} %get-tuple-element.11), channel_id=1, source_target_pairs={{0,4},{1,5},{2,6},{3,7},{4,32},{5,33},{6,34},{7,35},{32,36},{33,37... | collective-permute-start | bytes 1179656 | tf_op jit(solution)/shard_map/ppermute | solution.py:41
  54.8 1.0 copy-start.4
  57.6 48.9 %all-to-all-start.1 = ((bf16[16,96,896]{2,1,0:T(8,128)(2,1)}), bf16[16,96,896]{2,1,0:T(8,128)(2,1)S(1)}, u32[]{:S(2)}, u32[]{:S(2)}) async-start(bf16[16,96,896]{2,1,0:T(8,128)(2,1)} %shard_map.106), calls=%async_computation.1 | async-start | bytes 5505024 | tf_op jit(solution)/shard_map/all_to_all | solution.py:46
  64.5 15.4 %copy-start.5 = (s32[8]{0:T(128)S(1)}, s32[8]{0:T(128)}, u32[]{:S(2)}) copy-start(s32[8]{0:T(128)} %param.17) | copy-start | bytes 100
  64.5 25.4 %copy-start.6 = (f32[2,24]{1,0:T(2,128)S(1)}, f32[2,24]{1,0:T(2,128)}, u32[]{:S(2)}) copy-start(f32[2,24]{1,0:T(2,128)} %param.16) | copy-start | bytes 580
  67.2 54.2 %collective-permute-start.6 = (bf16[16,96,256]{2,1,0:T(8,128)(2,1)}, bf16[16,96,256]{2,1,0:T(8,128)(2,1)}, u32[]{:S(2)}, u32[]{:S(2)}) collective-permute-start(bf16[16,96,256]{2,1,0:T(8,128)(2,1)} %get-tuple-element.18), channel_id=1, source_target_pairs={{0,0},{1,1},{2,2},{3,3},{4,4},{5,5},{6,6},{7,7},{32,32},{33,33},{3... | collective-permute-start | bytes 2359304 | tf_op jit(solution)/shard_map/ppermute | solution.py:41
  74.6 48.5 %collective-permute-start.5 = (bf16[16,96,256]{2,1,0:T(8,128)(2,1)}, bf16[16,96,256]{2,1,0:T(8,128)(2,1)}, u32[]{:S(2)}, u32[]{:S(2)}) collective-permute-start(bf16[16,96,256]{2,1,0:T(8,128)(2,1)} %get-tuple-element.18), channel_id=1, source_target_pairs={{0,32},{1,33},{2,34},{3,35},{4,36},{5,37},{6,38},{7,39},{32,0},{33... | collective-permute-start | bytes 2359304 | tf_op jit(solution)/shard_map/ppermute | solution.py:41
  81.8 62.0 %collective-permute-start.4 = (bf16[16,96,256]{2,1,0:T(8,128)(2,1)}, bf16[16,96,256]{2,1,0:T(8,128)(2,1)}, u32[]{:S(2)}, u32[]{:S(2)}) collective-permute-start(bf16[16,96,256]{2,1,0:T(8,128)(2,1)} %get-tuple-element.19), channel_id=1, source_target_pairs={{0,0},{1,1},{2,2},{3,3},{4,4},{5,5},{6,6},{7,7},{32,32},{33,33},{3... | collective-permute-start | bytes 2359304 | tf_op jit(solution)/shard_map/ppermute | solution.py:41
  89.2 59.6 %collective-permute-start.3 = (bf16[16,96,256]{2,1,0:T(8,128)(2,1)}, bf16[16,96,256]{2,1,0:T(8,128)(2,1)}, u32[]{:S(2)}, u32[]{:S(2)}) collective-permute-start(bf16[16,96,256]{2,1,0:T(8,128)(2,1)} %get-tuple-element.19), channel_id=1, source_target_pairs={{0,32},{1,33},{2,34},{3,35},{4,36},{5,37},{6,38},{7,39},{32,0},{33... | collective-permute-start | bytes 2359304 | tf_op jit(solution)/shard_map/ppermute | solution.py:41
  117.4 17.5 %all-to-all-start.2 = ((bf16[16,96,128]{2,1,0:T(8,128)(2,1)}), bf16[16,96,128]{2,1,0:T(8,128)(2,1)S(1)}, u32[]{:S(2)}, u32[]{:S(2)}) async-start(bf16[16,96,128]{2,1,0:T(8,128)(2,1)} %bitcast.11), calls=%async_computation.2 | async-start | bytes 786432 | tf_op jit(solution)/shard_map/all_to_all | solution.py:46
  134.2 0.7 copy-start.2
  135.0 25.7 %all-to-all-start.4 = ((bf16[16,96,128]{2,1,0:T(8,128)(2,1)}), bf16[16,96,128]{2,1,0:T(8,128)(2,1)S(1)}, u32[]{:S(2)}, u32[]{:S(2)}) async-start(bf16[16,96,128]{2,1,0:T(8,128)(2,1)} %bitcast.28), calls=%async_computation.4 | async-start | bytes 786432 | tf_op jit(solution)/shard_map/all_to_all | solution.py:46
  159.9 0.7 copy-start.3

commit v3 on v2

v3 whole, which is shorter than its diff:
```python
import functools

import jax
import jax.numpy as jnp
import numpy as np
from jax import lax
from jax.experimental import pallas as pl
from jax.experimental.pallas import tpu as pltpu
from jax.sharding import PartitionSpec as P

HEADS = 24
HD = 128
TOP = 448.0
LOG2E = 1.4426950408889634

NY, NH, NX, NZ = 4, 2, 4, 4
SEATS = NY * NX
HALF = SEATS // 2
PER = HEADS // HALF
BOTH = ("seq", "tower")
VMEM_LIMIT = 32 * 1024 * 1024
PACK_LIMIT = 60 * 1024 * 1024


def z_route(pick):
    pairs = []
    around = NH * NZ
    for y in range(NY):
        for x in range(NX):
            for z in range(around):
                for core in range(2):

                    def device(at):
                        return (y * NH * NX + (at // NZ) * NX + x) * (2 * NZ) + (at % NZ) * 2 + core

                    pairs.append((device(z), device((z + pick(y * NX + x)) % around)))
    return pairs


def move(block, pick):
    return lax.ppermute(block, BOTH, z_route(pick))


def spread(block):
    groups = [[y * NH * NX + h * NX + x for y in range(NY) for x in range(NX)] for h in range(NH)]
    return lax.all_to_all(block, "seq", 0, 0, axis_index_groups=groups, tiled=True)


def attend_body(slope_ref, base_ref, q_ref, *refs, chunk):
    key_refs, value_refs = refs[:2], refs[2:4]
    out_ref, tile_ref, score_ref = refs[-3:]
    if len(refs) > 7:
        out_ref[:, :HD] = refs[4][...]
    slope = slope_ref[chunk]
    rows = q_ref.shape[0]
    run = tile_ref.shape[0]
    runs = rows // run
    scale = HD ** (-0.5) * LOG2E
    tile_ref[...] = (
        lax.broadcasted_iota(jnp.int32, (run, run), 0) - lax.broadcasted_iota(jnp.int32, (run, run), 1)
    ).astype(jnp.float32) * (slope / scale)
    for i in range(runs):
        own = slice(i * run, (i + 1) * run)
        peak = None
        for half, ref in enumerate(key_refs):
            for j in range(runs):
                scores = lax.dot_general(
                    q_ref[own, :], ref[j * run : (j + 1) * run, :], (((1,), (1,)), ((), ())),
                    preferred_element_type=jnp.float32,
                )
                base = ((i - j) * (2 * run) + base_ref[half]).astype(jnp.float32) * (slope / scale)
                scores = scores - jnp.abs(tile_ref[...] + base)
                at = (half * runs + j) * run
                score_ref[i % 2, :, at : at + run] = scores
                for lane in range(0, run, 128):
                    part = scores[:, lane : lane + 128]
                    peak = part if peak is None else jnp.maximum(peak, part)
        peak = jnp.max(peak, axis=1, keepdims=True) * scale
        total = jnp.zeros((run, 128), jnp.float32)
        out = jnp.zeros((run, HD), jnp.float32)
        for half, ref in enumerate(value_refs):
            for j in range(runs):
                at = (half * runs + j) * run
                weights = jnp.exp2(score_ref[i % 2, :, at : at + run] * scale - peak)
                for lane in range(0, run, 128):
                    total = total + weights[:, lane : lane + 128]
                out = out + jnp.dot(
                    weights.astype(jnp.bfloat16), ref[j * run : (j + 1) * run, :],
                    preferred_element_type=jnp.float32,
                )
        out_ref[own, -HD:] = (out / jnp.sum(total, axis=1, keepdims=True)).astype(jnp.bfloat16)


def attend(slopes, bases, queries, keys, values, chunk, beside=()):
    rows = queries.shape[0]
    run = rows // NY
    wide = HD * (1 + len(beside))

    def column(at):
        return pl.BlockSpec((rows, HD), lambda i: (0, at))

    return pl.pallas_call(
        functools.partial(attend_body, chunk=chunk),
        grid=(1,),
        in_specs=[pl.BlockSpec(memory_space=pltpu.SMEM)] * 2
        + [column(queries.shape[1] // HD - PER + chunk)]
        + [column(at) for _, at in keys + values]
        + [column(0) for _ in beside],
        out_specs=pl.BlockSpec((rows, wide), lambda i: (0, 0)),
        out_shape=jax.ShapeDtypeStruct((rows, wide), jnp.bfloat16),
        scratch_shapes=[pltpu.VMEM((run, run), jnp.float32), pltpu.VMEM((2, run, 2 * rows), jnp.float32)],
        compiler_params=pltpu.CompilerParams(vmem_limit_bytes=VMEM_LIMIT),
        cost_estimate=pl.CostEstimate(flops=rows * HD, bytes_accessed=rows * HD, transcendentals=0),
    )(slopes, bases, queries, *(a.reshape(rows, -1) for a, _ in keys + values), *beside)


def pack_body(exps_ref, *refs, items, outputs):
    out_refs = refs[len(refs) - outputs :]
    mine = out_refs[0]
    other = out_refs[1] if outputs > 1 else out_refs[0].at[HALF:]
    for n, (kind, chunk) in enumerate(items):
        self_ref, cross_ref = refs[2 * n : 2 * n + 2]
        to = slice(n * HD, (n + 1) * HD)
        for j in range(HALF):
            cols = slice(j * HD, (j + 1) * HD)
            mine[j, :, to] = self_ref[:, cols]
            block = cross_ref[:, cols]
            if kind is not None:
                power = jnp.full((1, HD), exps_ref[kind, chunk * HALF + j], jnp.int32)
                top = jnp.exp2(power.astype(jnp.float32)).astype(jnp.bfloat16).astype(jnp.float32) * TOP
                block = jnp.clip(block.astype(jnp.float32), -top, top).astype(jnp.bfloat16)
            other[j, :, to] = block


def pack(exps, pairs, items, apart=False):
    rows = pairs[0][0].shape[0]
    outputs, seats = (2, HALF) if apart else (1, SEATS)
    shape = (seats, rows, len(items) * HD)

    def slab(chunk):
        return pl.BlockSpec((rows, HALF * HD), lambda i: (0, chunk))

    return pl.pallas_call(
        functools.partial(pack_body, items=items, outputs=outputs),
        grid=(1,),
        in_specs=[pl.BlockSpec(memory_space=pltpu.SMEM)] + [slab(chunk) for _, chunk in items for _ in range(2)],
        out_specs=[pl.BlockSpec(shape, lambda i: (0, 0, 0))] * outputs,
        out_shape=[jax.ShapeDtypeStruct(shape, jnp.bfloat16)] * outputs,
        compiler_params=pltpu.CompilerParams(vmem_limit_bytes=PACK_LIMIT if len(items) < 5 else VMEM_LIMIT),
    )(exps, *(a for kind, _ in items for a in pairs[kind]))


def join_body(zs_ref, zm_ref, mine_ref, zp_ref, out_ref):
    for j in range(HALF):
        out_ref[j, :, :HD] = zs_ref[j]
        out_ref[HALF + j, :, :HD] = zm_ref[j]
        out_ref[j, :, HD:] = mine_ref[j]
        out_ref[HALF + j, :, HD:] = zp_ref[j]


def join(*arrays):
    _, rows, _ = arrays[0].shape
    shape = (SEATS, rows, 2 * HD)
    return pl.pallas_call(
        join_body,
        grid=(1,),
        in_specs=[pl.BlockSpec((HALF, rows, HD), lambda i: (0, 0, 0))] * 4,
        out_specs=pl.BlockSpec(shape, lambda i: (0, 0, 0)),
        out_shape=jax.ShapeDtypeStruct(shape, jnp.bfloat16),
        compiler_params=pltpu.CompilerParams(vmem_limit_bytes=VMEM_LIMIT),
        cost_estimate=pl.CostEstimate(flops=rows * HD, bytes_accessed=rows * HD, transcendentals=0),
    )(*arrays)


def unpack_body(*refs):
    self_ref, cross_ref = refs[-2:]
    chunk = 0
    for ref in refs[:-2]:
        for col in range(0, ref.shape[2], HD):
            for j in range(HALF):
                head = chunk * HALF + j
                cols = slice(head * HD, (head + 1) * HD)
                self_ref[:, cols] = ref[j, :, col : col + HD]
                cross_ref[:, cols] = ref[HALF + j, :, col : col + HD]
            chunk += 1


def unpack(*chunks):
    rows = chunks[0].shape[1]
    vmem = pl.BlockSpec(memory_space=pltpu.VMEM)
    return pl.pallas_call(
        unpack_body,
        in_specs=[vmem] * len(chunks),
        out_specs=[vmem] * 2,
        out_shape=[jax.ShapeDtypeStruct((rows, HEADS * HD), jnp.bfloat16)] * 2,
        compiler_params=pltpu.CompilerParams(vmem_limit_bytes=VMEM_LIMIT),
    )(*chunks)


def after(value, *others):
    return lax.optimization_barrier((value,) + others)[0]


def per_device(q_self, k_self, v_self, q_cross, k_cross, v_cross, scale_exps, cross_slopes, offsets):
    rows = q_self.shape[1]
    seat = lax.axis_index("seq")
    tower = lax.axis_index("tower")
    y, high, x = seat // (NH * NX), (seat // NX) % NH, seat % NX
    place = y * NX + x
    crossing = place >= HALF
    z = high * NZ + tower // 2
    towers = lax.axis_size("tower")
    partner = jnp.bitwise_xor(tower, towers // 2)

    modality = tower // (towers // 2)
    slopes = cross_slopes.reshape(2, PER, HALF)[modality, :, place % HALF]
    slopes = jnp.where(crossing, slopes * (LOG2E / (SEATS * NH * rows)), 0.0)
    shift = offsets[tower] - offsets[partner]
    run = NX * rows
    bases = jnp.stack(
        [(high - ((z + step) % (NH * NZ)) // NZ) * run + shift for step in (-2, 2)]
    ).astype(jnp.int32)

    def remote(seat_place):
        return NH * NZ // 2 if seat_place < HALF else 2

    def near(seat_place):
        return 0 if seat_place < HALF else -2

    exps = scale_exps[0]
    pairs = {0: (k_self[0], k_cross[0]), 1: (v_self[0], v_cross[0]), None: (q_self[0], q_cross[0])}
    mine, other = pack(exps, pairs, ((0, 0),), apart=True)
    zs = move(mine, lambda p: NH * NZ // 2)
    zm = move(other, lambda p: 2)
    zp = move(other, lambda p: -2)
    near_part = spread(pack(after(exps, mine), pairs, ((1, 0), (0, 1), (1, 1)))[0])
    far_part = pack(exps, pairs, ((0, 2), (1, 2), (None, 0), (None, 1), (None, 2)))[0]
    far_part = spread(after(far_part, near_part, zs, zm, zp))
    early = move(near_part, remote), move(near_part, near)
    joined = spread(after(join(zs, zm, mine, zp), far_part))
    block = far_part[:, :, : 2 * HD]
    late = move(after(block, joined, early[0]), remote), move(after(block, joined, early[1]), near)
    queries = far_part.reshape(SEATS * rows, -1)

    def shape(out):
        return out.reshape(SEATS, rows, -1)

    def halves(pair, at):
        return [(array, at) for array in pair]

    head = attend(slopes, bases, queries, [(joined, 0), (joined, 1)], halves(early, 0), 0)
    both = attend(slopes, bases, queries, halves(early, 1), halves(early, 2), 1, (head,))
    both_back = spread(after(shape(both), joined))
    tail = attend(after(slopes, both), bases, queries, halves(late, 0), halves(late, 1), 2)
    tail_back = spread(after(shape(tail), both_back))
    mine, other = unpack(both_back, tail_back)
    return mine[None], other[None]


def solution(mesh):
    split = P("tower", "seq", None)
    return jax.shard_map(
        per_device,
        mesh=mesh,
        in_specs=(split,) * 6 + (P("tower", None, None), P(), P()),
        out_specs=(split, split),
        check_vma=False,
    )
```

time: 178 us -> 171 us (0.961)
  waiting for transfers between devices: 54.3 us -> 43.7 us
  local copies, waits for them, and re-layouts: 5.82 us -> 12.2 us
  blocking collectives: 14.8 us -> 20.3 us
  Pallas kernels: 41.6 us -> 36.5 us
  starting transfers between devices: 56.7 us -> 54 us
    ppermute x7, waiting for transfers between devices: 37.9 us -> 9.56 us  [move(): return lax.ppermute(block, BOTH, z_route(pick))]
    all_to_all x4, waiting for transfers between devices: 16.3 us -> 34.2 us  [spread(): lax.all_to_all(block, 'seq', 0, 0, axis_index_groups=groups, tiled=True)]
    unnamed x14 -> x36, local copies, waits for them, and re-layouts: 2.5 us -> 10.6 us
    all_to_all x1, blocking collectives: 14.8 us -> 20.3 us  [spread(): lax.all_to_all(block, 'seq', 0, 0, axis_index_groups=groups, tiled=True)]
    pallas_call x7 -> x8, Pallas kernels: 41.6 us -> 36.5 us  [the longest x3 28.6 us: attend(): pl.pallas_call(functools.partial(attend_body, chunk=chunk), grid=(1,), in...]
    all_to_all x4, starting transfers between devices: 26.8 us -> 24.5 us  [spread(): lax.all_to_all(block, 'seq', 0, 0, axis_index_groups=groups, tiled=True)]
  transfers between devices with their start and end apart: 11 -> 11, of which waited for: 6 -> 5; matrix products, arithmetic and copies ran while one was open for 2% -> 1% of each run, Pallas kernels for 20% -> 17%
where the time goes in v3:
time: 171 us; the launch traced here: 169 us
  starting transfers between devices  54 us (32%)
  waiting for transfers between devices  43.7 us (26%)
  Pallas kernels  36.5 us (21%)
  blocking collectives  20.3 us (12%)
  local copies, waits for them, and re-layouts  12.2 us (7%)
  between operations  2.23 us (1%)
    all_to_all x4, waiting for transfers between devices, spread(): lax.all_to_all(block, 'seq', 0, 0, axis_index_groups=groups, tiled=True)  34.2 us
    ppermute x7, starting transfers between devices, move(): return lax.ppermute(block, BOTH, z_route(pick))  29.5 us
    pallas_call x3, Pallas kernels, attend(): pl.pallas_call(functools.partial(attend_body, chunk=chunk), grid=(1,), in...  28.6 us
    all_to_all x4, starting transfers between devices, spread(): lax.all_to_all(block, 'seq', 0, 0, axis_index_groups=groups, tiled=True)  24.5 us
    all_to_all x1, blocking collectives, spread(): lax.all_to_all(block, 'seq', 0, 0, axis_index_groups=groups, tiled=True)  20.3 us
    unnamed x36, local copies, waits for them, and re-layouts  10.6 us
    ppermute x7, waiting for transfers between devices, move(): return lax.ppermute(block, BOTH, z_route(pick))  9.56 us
    pallas_call x3, Pallas kernels, pack(): pl.pallas_call(functools.partial(pack_body, items=items, outputs=outputs)...  5.32 us
  transfers between devices with their start and end apart: 11, of which 5 were waited for; matrix products, arithmetic and copies ran while one was open for 1% of the time, Pallas kernels for 17%

profile of v3, /device:TPU:32, one launch (start us, length us, event | category | flops | bytes accessed | tf_op | source)
XLA Modules:
  0.0 169.3 jit_solution(9155998192340351416)
XLA Ops:
  0.6 1.8 %shard_map.105 = (bf16[8,96,128]{2,1,0:T(8,128)(2,1)}, bf16[8,96,128]{2,1,0:T(8,128)(2,1)}) custom-call(s32[2,24]{1,0:T(2,128)} %bitcast.46, bf16[96,3072]{1,0:T(8,128)(2,1)} %bitcast.38, bf16[96,3072]{1,0:T(8,128)(2,1)} %bitcast.41), custom_call_target="tpu_custom_call" | custom-call | tf_op jit(solution)/shard_map/pallas_call | solution.py:143
  2.4 2.6 %shard_map.106 = bf16[16,96,384]{2,1,0:T(8,128)(2,1)} custom-call(s32[2,24]{1,0:T(2,128)} %bitcast.47, bf16[96,3072]{1,0:T(8,128)(2,1)} %bitcast.26, bf16[96,3072]{1,0:T(8,128)(2,1)} %bitcast.29, bf16[96,3072]{1,0:T(8,128)(2,1)} %bitcast.39, bf16[96,3072]{1,0:T(8,128)(2,1)} %bitcast.42, bf16[96,3072]{1,0:T(8,128)(2,1)} %bitcast.27, bf16[96,3072]{1,0:T(8,128)(2,1)} %bitcast.30), custom_call_target="tpu_custom_call" | custom-call | tf_op jit(solution)/shard_map/pallas_call | solution.py:143
  5.1 7.2 %all-to-all-start = ((bf16[16,96,384]{2,1,0:T(8,128)(2,1)}), bf16[16,96,384]{2,1,0:T(8,128)(2,1)}, u32[]{:S(2)}, u32[]{:S(2)}) async-start(bf16[16,96,384]{2,1,0:T(8,128)(2,1)} %shard_map.106), calls=%async_computation | async-start | bytes 2359296 | tf_op jit(solution)/shard_map/all_to_all | solution.py:46
  12.3 6.4 %collective-permute-start = (bf16[8,96,128]{2,1,0:T(8,128)(2,1)S(1)}, bf16[8,96,128]{2,1,0:T(8,128)(2,1)S(1)}, u32[]{:S(2)}, u32[]{:S(2)}) collective-permute-start(bf16[8,96,128]{2,1,0:T(8,128)(2,1)S(1)} %copy-done.9), channel_id=1, source_target_pairs={{0,32},{1,33},{2,34},{3,35},{4,36},{5,37},{6,38},{7,39},{32,0},{33... | collective-permute-start | bytes 589832 | tf_op jit(solution)/shard_map/ppermute | solution.py:41
  18.7 1.5 collective-permute-start.1
  20.2 2.7 %collective-permute-start.2 = (bf16[8,96,128]{2,1,0:T(8,128)(2,1)S(1)}, bf16[8,96,128]{2,1,0:T(8,128)(2,1)S(1)}, u32[]{:S(2)}, u32[]{:S(2)}) collective-permute-start(bf16[8,96,128]{2,1,0:T(8,128)(2,1)S(1)} %copy-done.17), channel_id=1, source_target_pairs={{0,36},{1,37},{2,38},{3,39},{4,0},{5,1},{6,2},{7,3},{32,4},{33,5},... | collective-permute-start | bytes 589832 | tf_op jit(solution)/shard_map/ppermute | solution.py:41
  22.9 1.1 copy-done.1
  23.9 1.1 copy-done.2
  25.0 1.1 copy-done.3
  26.1 1.1 copy-done.4
  28.0 1.3 copy-done
  29.3 6.7 %collective-permute-done.1.zm_ref = bf16[8,96,128]{2,1,0:T(8,128)(2,1)S(1)} collective-permute-done((bf16[8,96,128]{2,1,0:T(8,128)(2,1)S(1)}, bf16[8,96,128]{2,1,0:T(8,128)(2,1)S(1)}, u32[]{:S(2)}, u32[]{:S(2)}) %collective-permute-start.1) | collective-permute-done | bytes 196640 | tf_op jit(solution)/shard_map/ppermute | solution.py:41
  37.4 6.9 %all-to-all-start.1 = ((bf16[16,96,640]{2,1,0:T(8,128)(2,1)}), bf16[16,96,640]{2,1,0:T(8,128)(2,1)S(1)}, u32[]{:S(2)}, u32[]{:S(2)}) async-start(bf16[16,96,640]{2,1,0:T(8,128)(2,1)} %copy-done), calls=%async_computation.1 | async-start | bytes 3932160 | tf_op jit(solution)/shard_map/all_to_all | solution.py:46
  44.3 1.9 %collective-permute-start.4 = (bf16[16,96,384]{2,1,0:T(8,128)(2,1)}, bf16[16,96,384]{2,1,0:T(8,128)(2,1)S(1)}, u32[]{:S(2)}, u32[]{:S(2)}) collective-permute-start(bf16[16,96,384]{2,1,0:T(8,128)(2,1)} %all-to-all-done), channel_id=1, source_target_pairs={{0,0},{1,1},{2,2},{3,3},{4,4},{5,5},{6,6},{7,7},{32,32},{33,33},{3... | collective-permute-start | bytes 3538952 | tf_op jit(solution)/shard_map/ppermute | solution.py:41
  46.2 4.8 %collective-permute-start.3 = (bf16[16,96,384]{2,1,0:T(8,128)(2,1)}, bf16[16,96,384]{2,1,0:T(8,128)(2,1)}, u32[]{:S(2)}, u32[]{:S(2)}) collective-permute-start(bf16[16,96,384]{2,1,0:T(8,128)(2,1)} %all-to-all-done), channel_id=1, source_target_pairs={{0,32},{1,33},{2,34},{3,35},{4,36},{5,37},{6,38},{7,39},{32,0},{33... | collective-permute-start | bytes 3538952 | tf_op jit(solution)/shard_map/ppermute | solution.py:41
  50.9 0.9 copy-done.11
  51.9 0.9 copy-done.13
  52.9 0.9 copy-done.8
  53.9 19.4 %all-to-all-done.1 = bf16[16,96,640]{2,1,0:T(8,128)(2,1)S(1)} async-done(((bf16[16,96,640]{2,1,0:T(8,128)(2,1)}), bf16[16,96,640]{2,1,0:T(8,128)(2,1)S(1)}, u32[]{:S(2)}, u32[]{:S(2)}) %all-to-all-start.1) | async-done | bytes 1966112 | tf_op jit(solution)/shard_map/all_to_all | solution.py:46
  73.2 4.3 %all-to-all-start.2 = ((bf16[16,96,256]{2,1,0:T(8,128)(2,1)}), bf16[16,96,256]{2,1,0:T(8,128)(2,1)}, u32[]{:S(2)}, u32[]{:S(2)}) async-start(bf16[16,96,256]{2,1,0:T(8,128)(2,1)} %copy-done.8), calls=%async_computation.2 | async-start | bytes 1572864 | tf_op jit(solution)/shard_map/all_to_all | solution.py:46
  79.6 1.0 slice.4
  80.5 10.6 %all-to-all-done.2 = bf16[16,96,256]{2,1,0:T(8,128)(2,1)} async-done(((bf16[16,96,256]{2,1,0:T(8,128)(2,1)}), bf16[16,96,256]{2,1,0:T(8,128)(2,1)}, u32[]{:S(2)}, u32[]{:S(2)}) %all-to-all-start.2) | async-done | bytes 786464 | tf_op jit(solution)/shard_map/all_to_all | solution.py:46
  91.2 7.4 %collective-permute-start.6 = (bf16[16,96,256]{2,1,0:T(8,128)(2,1)}, bf16[16,96,256]{2,1,0:T(8,128)(2,1)}, u32[]{:S(2)}, u32[]{:S(2)}) collective-permute-start(bf16[16,96,256]{2,1,0:T(8,128)(2,1)} %slice.4), channel_id=1, source_target_pairs={{0,0},{1,1},{2,2},{3,3},{4,4},{5,5},{6,6},{7,7},{32,32},{33,33},{3... | collective-permute-start | bytes 2359304 | tf_op jit(solution)/shard_map/ppermute | solution.py:41
  98.6 2.9 %collective-permute-done.3 = bf16[16,96,384]{2,1,0:T(8,128)(2,1)} collective-permute-done((bf16[16,96,384]{2,1,0:T(8,128)(2,1)}, bf16[16,96,384]{2,1,0:T(8,128)(2,1)}, u32[]{:S(2)}, u32[]{:S(2)}) %collective-permute-start.3) | collective-permute-done | bytes 1179680 | tf_op jit(solution)/shard_map/ppermute | solution.py:41
  101.5 4.9 %collective-permute-start.5 = (bf16[16,96,256]{2,1,0:T(8,128)(2,1)}, bf16[16,96,256]{2,1,0:T(8,128)(2,1)}, u32[]{:S(2)}, u32[]{:S(2)}) collective-permute-start(bf16[16,96,256]{2,1,0:T(8,128)(2,1)} %slice.4), channel_id=1, source_target_pairs={{0,32},{1,33},{2,34},{3,35},{4,36},{5,37},{6,38},{7,39},{32,0},{33... | collective-permute-start | bytes 2359304 | tf_op jit(solution)/shard_map/ppermute | solution.py:41
  106.7 9.4 %shard_map.108.refs_4_ = bf16[1536,128]{1,0:T(8,128)(2,1)S(1)} custom-call(f32[3]{0:T(128)S(1)} %select_reduce_fusion.slope_ref, s32[2]{0:T(128)S(1)} %pad_add_fusion.base_ref, bf16[1536,640]{1,0:T(8,128)(2,1)S(1)} %bitcast.20, bf16[1536,256]{1,0:T(8,128)(2,1)} %bitcast.13.refs_0_.refs_1_, bf16[1536,256]{1,0:T(8,128)(2,1)} %bitcast.13.refs_0_.refs_1_, ...), custom_call_target="tpu_custom_call" | custom-call | flops 196608 | bytes 196608 | tf_op jit(solution)/shard_map/pallas_call | solution.py:102
  116.1 9.7 %shard_map.109 = bf16[1536,256]{1,0:T(8,128)(2,1)S(1)} custom-call(f32[3]{0:T(128)S(1)} %select_reduce_fusion.slope_ref, s32[2]{0:T(128)S(1)} %pad_add_fusion.base_ref, bf16[1536,640]{1,0:T(8,128)(2,1)S(1)} %bitcast.21, bf16[1536,384]{1,0:T(8,128)(2,1)} %bitcast.11.refs_2_.refs_0_, bf16[1536,384]{1,0:T(8,128)(2,1)S(1)} %bitcast.24, ...), custom_call_target="tpu_custom_call" | custom-call | flops 196608 | bytes 196608 | tf_op jit(solution)/shard_map/pallas_call | solution.py:102
  126.7 6.1 %all-to-all-start.3 = ((bf16[16,96,256]{2,1,0:T(8,128)(2,1)}), bf16[16,96,256]{2,1,0:T(8,128)(2,1)}, u32[]{:S(2)}, u32[]{:S(2)}) async-start(bf16[16,96,256]{2,1,0:T(8,128)(2,1)} %bitcast.44), calls=%async_computation.3 | async-start | bytes 1572864 | tf_op jit(solution)/shard_map/all_to_all | solution.py:46
  132.9 9.5 %shard_map.110 = bf16[1536,128]{1,0:T(8,128)(2,1)S(1)} custom-call(f32[3]{0:T(128)S(1)} %select_reduce_fusion.slope_ref, s32[2]{0:T(128)S(1)} %pad_add_fusion.base_ref, bf16[1536,640]{1,0:T(8,128)(2,1)S(1)} %bitcast.22, bf16[1536,256]{1,0:T(8,128)(2,1)} %bitcast.15.refs_0_.refs_2_, bf16[1536,256]{1,0:T(8,128)(2,1)} %bitcast.16.refs_1_.refs_3_, ...), custom_call_target="tpu_custom_call" | custom-call | flops 196608 | bytes 196608 | tf_op jit(solution)/shard_map/pallas_call | solution.py:102
  142.4 4.1 %all-to-all-done.3.refs_0_ = bf16[16,96,256]{2,1,0:T(8,128)(2,1)} async-done(((bf16[16,96,256]{2,1,0:T(8,128)(2,1)}), bf16[16,96,256]{2,1,0:T(8,128)(2,1)}, u32[]{:S(2)}, u32[]{:S(2)}) %all-to-all-start.3) | async-done | bytes 786464 | tf_op jit(solution)/shard_map/all_to_all | solution.py:46
  146.5 20.3 %all_to_all.25.refs_1_ = bf16[16,96,128]{2,1,0:T(8,128)(2,1)S(1)} all-to-all(bf16[16,96,128]{2,1,0:T(8,128)(2,1)S(1)} %bitcast.45), channel_id=1, replica_groups={{0,8,16,24,64,72,80,88,128,136,144,152,192,200,208,216},{32,40,48,56,96..., dimensions={0} | all-to-all | bytes 786432 | tf_op jit(solution)/shard_map/all_to_all | solution.py:46
  166.8 2.5 %shard_map.111 = (bf16[96,3072]{1,0:T(8,128)(2,1)}, bf16[96,3072]{1,0:T(8,128)(2,1)}) custom-call(bf16[16,96,256]{2,1,0:T(8,128)(2,1)} %all-to-all-done.3.refs_0_, bf16[16,96,128]{2,1,0:T(8,128)(2,1)S(1)} %all_to_all.25.refs_1_), custom_call_target="tpu_custom_call" | custom-call | tf_op jit(solution)/shard_map/pallas_call | solution.py:191
  (40 shorter events, 4.3 us)
Async XLA Ops:
  5.1 7.3 %copy-start.9 = (bf16[8,96,128]{2,1,0:T(8,128)(2,1)S(1)}, bf16[8,96,128]{2,1,0:T(8,128)(2,1)}, u32[]{:S(2)}) copy-start(bf16[8,96,128]{2,1,0:T(8,128)(2,1)} %get-tuple-element.14.mine_ref) | copy-start | bytes 589828
  5.1 13.7 %copy-start.17 = (bf16[8,96,128]{2,1,0:T(8,128)(2,1)S(1)}, bf16[8,96,128]{2,1,0:T(8,128)(2,1)}, u32[]{:S(2)}) copy-start(bf16[8,96,128]{2,1,0:T(8,128)(2,1)} %get-tuple-element.16) | copy-start | bytes 589828
  5.1 17.8 %copy-start.5 = (bf16[1,96,3072]{2,1,0:T(8,128)(2,1)S(1)}, bf16[1,96,3072]{2,1,0:T(8,128)(2,1)}, u32[]{:S(2)}) copy-start(bf16[1,96,3072]{2,1,0:T(8,128)(2,1)} %param.10) | copy-start | bytes 1769476
  5.1 17.8 %copy-start.6 = (bf16[1,96,3072]{2,1,0:T(8,128)(2,1)S(1)}, bf16[1,96,3072]{2,1,0:T(8,128)(2,1)}, u32[]{:S(2)}) copy-start(bf16[1,96,3072]{2,1,0:T(8,128)(2,1)} %param.13) | copy-start | bytes 1769476
  5.1 17.8 %copy-start.14 = (s32[1,2,24]{2,1,0:T(2,128)S(1)}, s32[1,2,24]{2,1,0:T(2,128)}, u32[]{:S(2)}) copy-start(s32[1,2,24]{2,1,0:T(2,128)} %param.15) | copy-start | bytes 580
  5.1 32.3 %all-to-all-start = ((bf16[16,96,384]{2,1,0:T(8,128)(2,1)}), bf16[16,96,384]{2,1,0:T(8,128)(2,1)}, u32[]{:S(2)}, u32[]{:S(2)}) async-start(bf16[16,96,384]{2,1,0:T(8,128)(2,1)} %shard_map.106), calls=%async_computation | async-start | bytes 2359296 | tf_op jit(solution)/shard_map/all_to_all | solution.py:46
  12.3 17.0 %collective-permute-start = (bf16[8,96,128]{2,1,0:T(8,128)(2,1)S(1)}, bf16[8,96,128]{2,1,0:T(8,128)(2,1)S(1)}, u32[]{:S(2)}, u32[]{:S(2)}) collective-permute-start(bf16[8,96,128]{2,1,0:T(8,128)(2,1)S(1)} %copy-done.9), channel_id=1, source_target_pairs={{0,32},{1,33},{2,34},{3,35},{4,36},{5,37},{6,38},{7,39},{32,0},{33... | collective-permute-start | bytes 589832 | tf_op jit(solution)/shard_map/ppermute | solution.py:41
  18.7 17.3 %collective-permute-start.1 = (bf16[8,96,128]{2,1,0:T(8,128)(2,1)S(1)}, bf16[8,96,128]{2,1,0:T(8,128)(2,1)S(1)}, u32[]{:S(2)}, u32[]{:S(2)}) collective-permute-start(bf16[8,96,128]{2,1,0:T(8,128)(2,1)S(1)} %copy-done.17), channel_id=1, source_target_pairs={{0,4},{1,5},{2,6},{3,7},{4,32},{5,33},{6,34},{7,35},{32,36},{33,37... | collective-permute-start | bytes 589832 | tf_op jit(solution)/shard_map/ppermute | solution.py:41
  20.2 16.5 %collective-permute-start.2 = (bf16[8,96,128]{2,1,0:T(8,128)(2,1)S(1)}, bf16[8,96,128]{2,1,0:T(8,128)(2,1)S(1)}, u32[]{:S(2)}, u32[]{:S(2)}) collective-permute-start(bf16[8,96,128]{2,1,0:T(8,128)(2,1)S(1)} %copy-done.17), channel_id=1, source_target_pairs={{0,36},{1,37},{2,38},{3,39},{4,0},{5,1},{6,2},{7,3},{32,4},{33,5},... | collective-permute-start | bytes 589832 | tf_op jit(solution)/shard_map/ppermute | solution.py:41
  22.9 1.1 copy-start.1
  23.9 1.1 copy-start.2
  25.0 1.1 copy-start.3
  26.1 1.1 copy-start.4
  28.0 1.3 copy-start
  36.0 0.7 copy-start.10
  36.7 0.7 copy-start.12
  37.4 35.9 %all-to-all-start.1 = ((bf16[16,96,640]{2,1,0:T(8,128)(2,1)}), bf16[16,96,640]{2,1,0:T(8,128)(2,1)S(1)}, u32[]{:S(2)}, u32[]{:S(2)}) async-start(bf16[16,96,640]{2,1,0:T(8,128)(2,1)} %copy-done), calls=%async_computation.1 | async-start | bytes 3932160 | tf_op jit(solution)/shard_map/all_to_all | solution.py:46
  44.3 36.3 %collective-permute-start.4 = (bf16[16,96,384]{2,1,0:T(8,128)(2,1)}, bf16[16,96,384]{2,1,0:T(8,128)(2,1)S(1)}, u32[]{:S(2)}, u32[]{:S(2)}) collective-permute-start(bf16[16,96,384]{2,1,0:T(8,128)(2,1)} %all-to-all-done), channel_id=1, source_target_pairs={{0,0},{1,1},{2,2},{3,3},{4,4},{5,5},{6,6},{7,7},{32,32},{33,33},{3... | collective-permute-start | bytes 3538952 | tf_op jit(solution)/shard_map/ppermute | solution.py:41
  46.2 55.3 %collective-permute-start.3 = (bf16[16,96,384]{2,1,0:T(8,128)(2,1)}, bf16[16,96,384]{2,1,0:T(8,128)(2,1)}, u32[]{:S(2)}, u32[]{:S(2)}) collective-permute-start(bf16[16,96,384]{2,1,0:T(8,128)(2,1)} %all-to-all-done), channel_id=1, source_target_pairs={{0,32},{1,33},{2,34},{3,35},{4,36},{5,37},{6,38},{7,39},{32,0},{33... | collective-permute-start | bytes 3538952 | tf_op jit(solution)/shard_map/ppermute | solution.py:41
  50.9 0.9 copy-start.11
  51.9 0.9 copy-start.13
  52.9 0.9 copy-start.8
  53.9 23.8 %copy-start.15 = (s32[8]{0:T(128)S(1)}, s32[8]{0:T(128)}, u32[]{:S(2)}) copy-start(s32[8]{0:T(128)} %param.17) | copy-start | bytes 100
  73.2 17.9 %all-to-all-start.2 = ((bf16[16,96,256]{2,1,0:T(8,128)(2,1)}), bf16[16,96,256]{2,1,0:T(8,128)(2,1)}, u32[]{:S(2)}, u32[]{:S(2)}) async-start(bf16[16,96,256]{2,1,0:T(8,128)(2,1)} %copy-done.8), calls=%async_computation.2 | async-start | bytes 1572864 | tf_op jit(solution)/shard_map/all_to_all | solution.py:46
  77.5 28.9 %copy-start.16 = (f32[2,24]{1,0:T(2,128)S(1)}, f32[2,24]{1,0:T(2,128)}, u32[]{:S(2)}) copy-start(f32[2,24]{1,0:T(2,128)} %param.16) | copy-start | bytes 580
  91.2 41.7 %collective-permute-start.6 = (bf16[16,96,256]{2,1,0:T(8,128)(2,1)}, bf16[16,96,256]{2,1,0:T(8,128)(2,1)}, u32[]{:S(2)}, u32[]{:S(2)}) collective-permute-start(bf16[16,96,256]{2,1,0:T(8,128)(2,1)} %slice.4), channel_id=1, source_target_pairs={{0,0},{1,1},{2,2},{3,3},{4,4},{5,5},{6,6},{7,7},{32,32},{33,33},{3... | collective-permute-start | bytes 2359304 | tf_op jit(solution)/shard_map/ppermute | solution.py:41
  101.5 31.4 %collective-permute-start.5 = (bf16[16,96,256]{2,1,0:T(8,128)(2,1)}, bf16[16,96,256]{2,1,0:T(8,128)(2,1)}, u32[]{:S(2)}, u32[]{:S(2)}) collective-permute-start(bf16[16,96,256]{2,1,0:T(8,128)(2,1)} %slice.4), channel_id=1, source_target_pairs={{0,32},{1,33},{2,34},{3,35},{4,36},{5,37},{6,38},{7,39},{32,0},{33... | collective-permute-start | bytes 2359304 | tf_op jit(solution)/shard_map/ppermute | solution.py:41
  125.8 0.9 copy-start.7
  126.7 19.8 %all-to-all-start.3 = ((bf16[16,96,256]{2,1,0:T(8,128)(2,1)}), bf16[16,96,256]{2,1,0:T(8,128)(2,1)}, u32[]{:S(2)}, u32[]{:S(2)}) async-start(bf16[16,96,256]{2,1,0:T(8,128)(2,1)} %bitcast.44), calls=%async_computation.3 | async-start | bytes 1572864 | tf_op jit(solution)/shard_map/all_to_all | solution.py:46

commit v4 on v3

--- a/solution.py
+++ b/solution.py
@@ -18,7 +18,7 @@
 HALF = SEATS // 2
 PER = HEADS // HALF
 BOTH = ("seq", "tower")
-VMEM_LIMIT = 32 * 1024 * 1024
+VMEM_LIMIT = 20 * 1024 * 1024
 PACK_LIMIT = 60 * 1024 * 1024
 
 
@@ -172,29 +172,27 @@
     )(*arrays)
 
 
-def unpack_body(*refs):
+def unpack_body(back_ref, *refs):
     self_ref, cross_ref = refs[-2:]
-    chunk = 0
-    for ref in refs[:-2]:
-        for col in range(0, ref.shape[2], HD):
-            for j in range(HALF):
-                head = chunk * HALF + j
-                cols = slice(head * HD, (head + 1) * HD)
-                self_ref[:, cols] = ref[j, :, col : col + HD]
-                cross_ref[:, cols] = ref[HALF + j, :, col : col + HD]
-            chunk += 1
-
-
-def unpack(*chunks):
-    rows = chunks[0].shape[1]
-    vmem = pl.BlockSpec(memory_space=pltpu.VMEM)
+    for c in range(back_ref.shape[2] // HD):
+        for j in range(HALF):
+            cols = slice((c * HALF + j) * HD, (c * HALF + j + 1) * HD)
+            self_ref[:, cols] = back_ref[j, :, c * HD : (c + 1) * HD]
+            cross_ref[:, cols] = back_ref[HALF + j, :, c * HD : (c + 1) * HD]
+
+
+def unpack(back, at, partial=()):
+    _, rows, wide = back.shape
     return pl.pallas_call(
         unpack_body,
-        in_specs=[vmem] * len(chunks),
-        out_specs=[vmem] * 2,
+        grid=(1,),
+        in_specs=[pl.BlockSpec(back.shape, lambda i: (0, 0, 0))] + [pl.BlockSpec(memory_space=pl.ANY)] * len(partial),
+        out_specs=[pl.BlockSpec((rows, wide * HALF), lambda i: (0, at))] * 2,
         out_shape=[jax.ShapeDtypeStruct((rows, HEADS * HD), jnp.bfloat16)] * 2,
+        input_output_aliases={1: 0, 2: 1} if partial else {},
         compiler_params=pltpu.CompilerParams(vmem_limit_bytes=VMEM_LIMIT),
-    )(*chunks)
+        cost_estimate=pl.CostEstimate(flops=rows * HD, bytes_accessed=rows * HD, transcendentals=0),
+    )(back, *partial)
 
 
 def after(value, *others):
@@ -253,7 +251,7 @@
     both_back = spread(after(shape(both), joined))
     tail = attend(after(slopes, both), bases, queries, halves(late, 0), halves(late, 1), 2)
     tail_back = spread(after(shape(tail), both_back))
-    mine, other = unpack(both_back, tail_back)
+    mine, other = unpack(tail_back, PER - 1, unpack(both_back, 0))
     return mine[None], other[None]
 
 

time: 171 us -> 172 us (level)
  blocking collectives: 20.3 us -> 0 us
  starting transfers between devices: 54 us -> 71 us
  waiting for transfers between devices: 43.7 us -> 45.8 us
    all_to_all x1 -> x0, blocking collectives: 20.3 us -> none  [spread(): lax.all_to_all(block, 'seq', 0, 0, axis_index_groups=groups, tiled=True)]
    ppermute x7, waiting for transfers between devices: 9.56 us -> 25.6 us  [move(): return lax.ppermute(block, BOTH, z_route(pick))]
    all_to_all x4 -> x5, waiting for transfers between devices: 34.2 us -> 20.2 us  [spread(): lax.all_to_all(block, 'seq', 0, 0, axis_index_groups=groups, tiled=True)]
    ppermute x7, starting transfers between devices: 29.5 us -> 38.1 us  [move(): return lax.ppermute(block, BOTH, z_route(pick))]
    all_to_all x4 -> x5, starting transfers between devices: 24.5 us -> 32.9 us  [spread(): lax.all_to_all(block, 'seq', 0, 0, axis_index_groups=groups, tiled=True)]
  transfers between devices with their start and end apart: 11 -> 12, of which waited for: 5 -> 5; matrix products, arithmetic and copies ran while one was open for 1% -> 1% of each run, Pallas kernels for 17% -> 19%
where the time goes in v4:
time: 172 us; the launch traced here: 169 us
  starting transfers between devices  71 us (41%)
  waiting for transfers between devices  45.8 us (27%)
  Pallas kernels  38 us (22%)
  local copies, waits for them, and re-layouts  12.2 us (7%)
  between operations  2.23 us (1%)
    ppermute x7, starting transfers between devices, move(): return lax.ppermute(block, BOTH, z_route(pick))  38.1 us
    all_to_all x5, starting transfers between devices, spread(): lax.all_to_all(block, 'seq', 0, 0, axis_index_groups=groups, tiled=True)  32.9 us
    pallas_call x3, Pallas kernels, attend(): pl.pallas_call(functools.partial(attend_body, chunk=chunk), grid=(1,), in...  29.5 us
    ppermute x7, waiting for transfers between devices, move(): return lax.ppermute(block, BOTH, z_route(pick))  25.6 us
    all_to_all x5, waiting for transfers between devices, spread(): lax.all_to_all(block, 'seq', 0, 0, axis_index_groups=groups, tiled=True)  20.2 us
    unnamed x36, local copies, waits for them, and re-layouts  10.6 us
    pallas_call x3, Pallas kernels, pack(): pl.pallas_call(functools.partial(pack_body, items=items, outputs=outputs)...  5.31 us
  transfers between devices with their start and end apart: 12, of which 5 were waited for; matrix products, arithmetic and copies ran while one was open for 1% of the time, Pallas kernels for 19%

profile of v4, /device:TPU:32, one launch (start us, length us, event | category | flops | bytes accessed | tf_op | source)
XLA Modules:
  0.0 169.5 jit_solution(14889866124106021499)
XLA Ops:
  0.6 1.8 %shard_map.105 = (bf16[8,96,128]{2,1,0:T(8,128)(2,1)}, bf16[8,96,128]{2,1,0:T(8,128)(2,1)}) custom-call(s32[2,24]{1,0:T(2,128)} %bitcast.45, bf16[96,3072]{1,0:T(8,128)(2,1)} %bitcast.38, bf16[96,3072]{1,0:T(8,128)(2,1)} %bitcast.41), custom_call_target="tpu_custom_call" | custom-call | tf_op jit(solution)/shard_map/pallas_call | solution.py:143
  2.4 2.6 %shard_map.106 = bf16[16,96,384]{2,1,0:T(8,128)(2,1)} custom-call(s32[2,24]{1,0:T(2,128)} %bitcast.46, bf16[96,3072]{1,0:T(8,128)(2,1)} %bitcast.26, bf16[96,3072]{1,0:T(8,128)(2,1)} %bitcast.29, bf16[96,3072]{1,0:T(8,128)(2,1)} %bitcast.39, bf16[96,3072]{1,0:T(8,128)(2,1)} %bitcast.42, bf16[96,3072]{1,0:T(8,128)(2,1)} %bitcast.27, bf16[96,3072]{1,0:T(8,128)(2,1)} %bitcast.30), custom_call_target="tpu_custom_call" | custom-call | tf_op jit(solution)/shard_map/pallas_call | solution.py:143
  5.1 7.2 %all-to-all-start = ((bf16[16,96,384]{2,1,0:T(8,128)(2,1)}), bf16[16,96,384]{2,1,0:T(8,128)(2,1)}, u32[]{:S(2)}, u32[]{:S(2)}) async-start(bf16[16,96,384]{2,1,0:T(8,128)(2,1)} %shard_map.106), calls=%async_computation | async-start | bytes 2359296 | tf_op jit(solution)/shard_map/all_to_all | solution.py:46
  12.3 6.4 %collective-permute-start = (bf16[8,96,128]{2,1,0:T(8,128)(2,1)S(1)}, bf16[8,96,128]{2,1,0:T(8,128)(2,1)S(1)}, u32[]{:S(2)}, u32[]{:S(2)}) collective-permute-start(bf16[8,96,128]{2,1,0:T(8,128)(2,1)S(1)} %copy-done.9), channel_id=1, source_target_pairs={{0,32},{1,33},{2,34},{3,35},{4,36},{5,37},{6,38},{7,39},{32,0},{33... | collective-permute-start | bytes 589832 | tf_op jit(solution)/shard_map/ppermute | solution.py:41
  18.7 1.5 collective-permute-start.1
  20.2 2.7 %collective-permute-start.2 = (bf16[8,96,128]{2,1,0:T(8,128)(2,1)S(1)}, bf16[8,96,128]{2,1,0:T(8,128)(2,1)S(1)}, u32[]{:S(2)}, u32[]{:S(2)}) collective-permute-start(bf16[8,96,128]{2,1,0:T(8,128)(2,1)S(1)} %copy-done.17), channel_id=1, source_target_pairs={{0,36},{1,37},{2,38},{3,39},{4,0},{5,1},{6,2},{7,3},{32,4},{33,5},... | collective-permute-start | bytes 589832 | tf_op jit(solution)/shard_map/ppermute | solution.py:41
  22.9 1.1 copy-done.1
  23.9 1.1 copy-done.2
  25.0 1.1 copy-done.3
  26.1 1.1 copy-done.4
  28.0 1.3 copy-done
  29.3 6.7 %collective-permute-done.1.zm_ref = bf16[8,96,128]{2,1,0:T(8,128)(2,1)S(1)} collective-permute-done((bf16[8,96,128]{2,1,0:T(8,128)(2,1)S(1)}, bf16[8,96,128]{2,1,0:T(8,128)(2,1)S(1)}, u32[]{:S(2)}, u32[]{:S(2)}) %collective-permute-start.1) | collective-permute-done | bytes 196640 | tf_op jit(solution)/shard_map/ppermute | solution.py:41
  37.3 6.9 %all-to-all-start.1 = ((bf16[16,96,640]{2,1,0:T(8,128)(2,1)}), bf16[16,96,640]{2,1,0:T(8,128)(2,1)S(1)}, u32[]{:S(2)}, u32[]{:S(2)}) async-start(bf16[16,96,640]{2,1,0:T(8,128)(2,1)} %copy-done), calls=%async_computation.1 | async-start | bytes 3932160 | tf_op jit(solution)/shard_map/all_to_all | solution.py:46
  44.2 4.8 %collective-permute-start.3 = (bf16[16,96,384]{2,1,0:T(8,128)(2,1)}, bf16[16,96,384]{2,1,0:T(8,128)(2,1)S(1)}, u32[]{:S(2)}, u32[]{:S(2)}) collective-permute-start(bf16[16,96,384]{2,1,0:T(8,128)(2,1)} %all-to-all-done), channel_id=1, source_target_pairs={{0,32},{1,33},{2,34},{3,35},{4,36},{5,37},{6,38},{7,39},{32,0},{33... | collective-permute-start | bytes 3538952 | tf_op jit(solution)/shard_map/ppermute | solution.py:41
  49.1 10.4 %collective-permute-start.4 = (bf16[16,96,384]{2,1,0:T(8,128)(2,1)}, bf16[16,96,384]{2,1,0:T(8,128)(2,1)}, u32[]{:S(2)}, u32[]{:S(2)}) collective-permute-start(bf16[16,96,384]{2,1,0:T(8,128)(2,1)} %all-to-all-done), channel_id=1, source_target_pairs={{0,0},{1,1},{2,2},{3,3},{4,4},{5,5},{6,6},{7,7},{32,32},{33,33},{3... | collective-permute-start | bytes 3538952 | tf_op jit(solution)/shard_map/ppermute | solution.py:41
  59.4 0.9 copy-done.11
  60.4 0.9 copy-done.13
  61.4 0.9 copy-done.8
  62.3 10.9 %all-to-all-done.1 = bf16[16,96,640]{2,1,0:T(8,128)(2,1)S(1)} async-done(((bf16[16,96,640]{2,1,0:T(8,128)(2,1)}), bf16[16,96,640]{2,1,0:T(8,128)(2,1)S(1)}, u32[]{:S(2)}, u32[]{:S(2)}) %all-to-all-start.1) | async-done | bytes 1966112 | tf_op jit(solution)/shard_map/all_to_all | solution.py:46
  73.2 4.3 %all-to-all-start.2 = ((bf16[16,96,256]{2,1,0:T(8,128)(2,1)}), bf16[16,96,256]{2,1,0:T(8,128)(2,1)}, u32[]{:S(2)}, u32[]{:S(2)}) async-start(bf16[16,96,256]{2,1,0:T(8,128)(2,1)} %copy-done.8), calls=%async_computation.2 | async-start | bytes 1572864 | tf_op jit(solution)/shard_map/all_to_all | solution.py:46
  79.6 1.0 slice.4
  80.5 18.9 %collective-permute-done.3 = bf16[16,96,384]{2,1,0:T(8,128)(2,1)S(1)} collective-permute-done((bf16[16,96,384]{2,1,0:T(8,128)(2,1)}, bf16[16,96,384]{2,1,0:T(8,128)(2,1)S(1)}, u32[]{:S(2)}, u32[]{:S(2)}) %collective-permute-start.3) | collective-permute-done | bytes 1179680 | tf_op jit(solution)/shard_map/ppermute | solution.py:41
  99.4 5.0 %collective-permute-start.5 = (bf16[16,96,256]{2,1,0:T(8,128)(2,1)}, bf16[16,96,256]{2,1,0:T(8,128)(2,1)}, u32[]{:S(2)}, u32[]{:S(2)}) collective-permute-start(bf16[16,96,256]{2,1,0:T(8,128)(2,1)} %slice.4), channel_id=1, source_target_pairs={{0,32},{1,33},{2,34},{3,35},{4,36},{5,37},{6,38},{7,39},{32,0},{33... | collective-permute-start | bytes 2359304 | tf_op jit(solution)/shard_map/ppermute | solution.py:41
  104.4 7.4 %collective-permute-start.6 = (bf16[16,96,256]{2,1,0:T(8,128)(2,1)}, bf16[16,96,256]{2,1,0:T(8,128)(2,1)}, u32[]{:S(2)}, u32[]{:S(2)}) collective-permute-start(bf16[16,96,256]{2,1,0:T(8,128)(2,1)} %slice.4), channel_id=1, source_target_pairs={{0,0},{1,1},{2,2},{3,3},{4,4},{5,5},{6,6},{7,7},{32,32},{33,33},{3... | collective-permute-start | bytes 2359304 | tf_op jit(solution)/shard_map/ppermute | solution.py:41
  112.2 9.4 %shard_map.108.refs_4_ = bf16[1536,128]{1,0:T(8,128)(2,1)S(1)} custom-call(f32[3]{0:T(128)S(1)} %select_reduce_fusion.slope_ref, s32[2]{0:T(128)S(1)} %pad_add_fusion.base_ref, bf16[1536,640]{1,0:T(8,128)(2,1)S(1)} %bitcast.20, bf16[1536,256]{1,0:T(8,128)(2,1)} %bitcast.13.refs_0_.refs_1_, bf16[1536,256]{1,0:T(8,128)(2,1)} %bitcast.13.refs_0_.refs_1_, ...), custom_call_target="tpu_custom_call" | custom-call | flops 196608 | bytes 196608 | tf_op jit(solution)/shard_map/pallas_call | solution.py:102
  121.6 9.7 %shard_map.109 = bf16[1536,256]{1,0:T(8,128)(2,1)S(1)} custom-call(f32[3]{0:T(128)S(1)} %select_reduce_fusion.slope_ref, s32[2]{0:T(128)S(1)} %pad_add_fusion.base_ref, bf16[1536,640]{1,0:T(8,128)(2,1)S(1)} %bitcast.21, bf16[1536,384]{1,0:T(8,128)(2,1)S(1)} %bitcast.24, bf16[1536,384]{1,0:T(8,128)(2,1)} %bitcast.12.refs_3_.refs_1_, ...), custom_call_target="tpu_custom_call" | custom-call | flops 196608 | bytes 196608 | tf_op jit(solution)/shard_map/pallas_call | solution.py:102
  132.2 5.4 %all-to-all-start.3 = ((bf16[16,96,256]{2,1,0:T(8,128)(2,1)}), bf16[16,96,256]{2,1,0:T(8,128)(2,1)}, u32[]{:S(2)}, u32[]{:S(2)}) async-start(bf16[16,96,256]{2,1,0:T(8,128)(2,1)} %bitcast.44), calls=%async_computation.3 | async-start | bytes 1572864 | tf_op jit(solution)/shard_map/all_to_all | solution.py:46
  137.7 10.3 %shard_map.110 = bf16[1536,128]{1,0:T(8,128)(2,1)} custom-call(f32[3]{0:T(128)S(1)} %select_reduce_fusion.slope_ref, s32[2]{0:T(128)S(1)} %pad_add_fusion.base_ref, bf16[1536,640]{1,0:T(8,128)(2,1)S(1)} %bitcast.22, bf16[1536,256]{1,0:T(8,128)(2,1)} %bitcast.14.refs_0_.refs_2_, bf16[1536,256]{1,0:T(8,128)(2,1)} %bitcast.15.refs_1_.refs_3_, ...), custom_call_target="tpu_custom_call" | custom-call | flops 196608 | bytes 196608 | tf_op jit(solution)/shard_map/pallas_call | solution.py:102
  148.0 1.3 all-to-all-done.3.back_ref
  149.3 9.1 %all-to-all-start.4 = ((bf16[16,96,128]{2,1,0:T(8,128)(2,1)}), bf16[16,96,128]{2,1,0:T(8,128)(2,1)S(1)}, u32[]{:S(2)}, u32[]{:S(2)}) async-start(bf16[16,96,128]{2,1,0:T(8,128)(2,1)} %bitcast.16), calls=%async_computation.4 | async-start | bytes 786432 | tf_op jit(solution)/shard_map/all_to_all | solution.py:46
  158.4 2.2 %shard_map.111 = (bf16[96,3072]{1,0:T(8,128)(2,1)}, bf16[96,3072]{1,0:T(8,128)(2,1)}) custom-call(bf16[16,96,256]{2,1,0:T(8,128)(2,1)} %all-to-all-done.3.back_ref), custom_call_target="tpu_custom_call" | custom-call | flops 12288 | bytes 12288 | tf_op jit(solution)/shard_map/pallas_call | solution.py:186
  160.6 8.0 %all-to-all-done.4.back_ref = bf16[16,96,128]{2,1,0:T(8,128)(2,1)S(1)} async-done(((bf16[16,96,128]{2,1,0:T(8,128)(2,1)}), bf16[16,96,128]{2,1,0:T(8,128)(2,1)S(1)}, u32[]{:S(2)}, u32[]{:S(2)}) %all-to-all-start.4) | async-done | bytes 393248 | tf_op jit(solution)/shard_map/all_to_all | solution.py:46
  (42 shorter events, 5.1 us)
Async XLA Ops:
  5.1 7.3 %copy-start.9 = (bf16[8,96,128]{2,1,0:T(8,128)(2,1)S(1)}, bf16[8,96,128]{2,1,0:T(8,128)(2,1)}, u32[]{:S(2)}) copy-start(bf16[8,96,128]{2,1,0:T(8,128)(2,1)} %get-tuple-element.16.mine_ref) | copy-start | bytes 589828
  5.1 13.7 %copy-start.17 = (bf16[8,96,128]{2,1,0:T(8,128)(2,1)S(1)}, bf16[8,96,128]{2,1,0:T(8,128)(2,1)}, u32[]{:S(2)}) copy-start(bf16[8,96,128]{2,1,0:T(8,128)(2,1)} %get-tuple-element.18) | copy-start | bytes 589828
  5.1 17.8 %copy-start.5 = (bf16[1,96,3072]{2,1,0:T(8,128)(2,1)S(1)}, bf16[1,96,3072]{2,1,0:T(8,128)(2,1)}, u32[]{:S(2)}) copy-start(bf16[1,96,3072]{2,1,0:T(8,128)(2,1)} %param.10) | copy-start | bytes 1769476
  5.1 17.8 %copy-start.6 = (bf16[1,96,3072]{2,1,0:T(8,128)(2,1)S(1)}, bf16[1,96,3072]{2,1,0:T(8,128)(2,1)}, u32[]{:S(2)}) copy-start(bf16[1,96,3072]{2,1,0:T(8,128)(2,1)} %param.13) | copy-start | bytes 1769476
  5.1 17.8 %copy-start.14 = (s32[1,2,24]{2,1,0:T(2,128)S(1)}, s32[1,2,24]{2,1,0:T(2,128)}, u32[]{:S(2)}) copy-start(s32[1,2,24]{2,1,0:T(2,128)} %param.15) | copy-start | bytes 580
  5.1 32.3 %all-to-all-start = ((bf16[16,96,384]{2,1,0:T(8,128)(2,1)}), bf16[16,96,384]{2,1,0:T(8,128)(2,1)}, u32[]{:S(2)}, u32[]{:S(2)}) async-start(bf16[16,96,384]{2,1,0:T(8,128)(2,1)} %shard_map.106), calls=%async_computation | async-start | bytes 2359296 | tf_op jit(solution)/shard_map/all_to_all | solution.py:46
  12.3 17.0 %collective-permute-start = (bf16[8,96,128]{2,1,0:T(8,128)(2,1)S(1)}, bf16[8,96,128]{2,1,0:T(8,128)(2,1)S(1)}, u32[]{:S(2)}, u32[]{:S(2)}) collective-permute-start(bf16[8,96,128]{2,1,0:T(8,128)(2,1)S(1)} %copy-done.9), channel_id=1, source_target_pairs={{0,32},{1,33},{2,34},{3,35},{4,36},{5,37},{6,38},{7,39},{32,0},{33... | collective-permute-start | bytes 589832 | tf_op jit(solution)/shard_map/ppermute | solution.py:41
  18.7 17.3 %collective-permute-start.1 = (bf16[8,96,128]{2,1,0:T(8,128)(2,1)S(1)}, bf16[8,96,128]{2,1,0:T(8,128)(2,1)S(1)}, u32[]{:S(2)}, u32[]{:S(2)}) collective-permute-start(bf16[8,96,128]{2,1,0:T(8,128)(2,1)S(1)} %copy-done.17), channel_id=1, source_target_pairs={{0,4},{1,5},{2,6},{3,7},{4,32},{5,33},{6,34},{7,35},{32,36},{33,37... | collective-permute-start | bytes 589832 | tf_op jit(solution)/shard_map/ppermute | solution.py:41
  20.2 16.5 %collective-permute-start.2 = (bf16[8,96,128]{2,1,0:T(8,128)(2,1)S(1)}, bf16[8,96,128]{2,1,0:T(8,128)(2,1)S(1)}, u32[]{:S(2)}, u32[]{:S(2)}) collective-permute-start(bf16[8,96,128]{2,1,0:T(8,128)(2,1)S(1)} %copy-done.17), channel_id=1, source_target_pairs={{0,36},{1,37},{2,38},{3,39},{4,0},{5,1},{6,2},{7,3},{32,4},{33,5},... | collective-permute-start | bytes 589832 | tf_op jit(solution)/shard_map/ppermute | solution.py:41
  22.9 1.1 copy-start.1
  23.9 1.1 copy-start.2
  25.0 1.1 copy-start.3
  26.1 1.1 copy-start.4
  28.0 1.3 copy-start
  36.0 0.7 copy-start.10
  36.7 0.7 copy-start.12
  37.3 35.9 %all-to-all-start.1 = ((bf16[16,96,640]{2,1,0:T(8,128)(2,1)}), bf16[16,96,640]{2,1,0:T(8,128)(2,1)S(1)}, u32[]{:S(2)}, u32[]{:S(2)}) async-start(bf16[16,96,640]{2,1,0:T(8,128)(2,1)} %copy-done), calls=%async_computation.1 | async-start | bytes 3932160 | tf_op jit(solution)/shard_map/all_to_all | solution.py:46
  44.2 55.2 %collective-permute-start.3 = (bf16[16,96,384]{2,1,0:T(8,128)(2,1)}, bf16[16,96,384]{2,1,0:T(8,128)(2,1)S(1)}, u32[]{:S(2)}, u32[]{:S(2)}) collective-permute-start(bf16[16,96,384]{2,1,0:T(8,128)(2,1)} %all-to-all-done), channel_id=1, source_target_pairs={{0,32},{1,33},{2,34},{3,35},{4,36},{5,37},{6,38},{7,39},{32,0},{33... | collective-permute-start | bytes 3538952 | tf_op jit(solution)/shard_map/ppermute | solution.py:41
  49.1 55.3 %collective-permute-start.4 = (bf16[16,96,384]{2,1,0:T(8,128)(2,1)}, bf16[16,96,384]{2,1,0:T(8,128)(2,1)}, u32[]{:S(2)}, u32[]{:S(2)}) collective-permute-start(bf16[16,96,384]{2,1,0:T(8,128)(2,1)} %all-to-all-done), channel_id=1, source_target_pairs={{0,0},{1,1},{2,2},{3,3},{4,4},{5,5},{6,6},{7,7},{32,32},{33,33},{3... | collective-permute-start | bytes 3538952 | tf_op jit(solution)/shard_map/ppermute | solution.py:41
  59.4 0.9 copy-start.11
  60.4 0.9 copy-start.13
  61.4 0.9 copy-start.8
  62.3 15.3 %copy-start.15 = (s32[8]{0:T(128)S(1)}, s32[8]{0:T(128)}, u32[]{:S(2)}) copy-start(s32[8]{0:T(128)} %param.17) | copy-start | bytes 100
  73.2 26.2 %all-to-all-start.2 = ((bf16[16,96,256]{2,1,0:T(8,128)(2,1)}), bf16[16,96,256]{2,1,0:T(8,128)(2,1)}, u32[]{:S(2)}, u32[]{:S(2)}) async-start(bf16[16,96,256]{2,1,0:T(8,128)(2,1)} %copy-done.8), calls=%async_computation.2 | async-start | bytes 1572864 | tf_op jit(solution)/shard_map/all_to_all | solution.py:46
  77.5 34.4 %copy-start.16 = (f32[2,24]{1,0:T(2,128)S(1)}, f32[2,24]{1,0:T(2,128)}, u32[]{:S(2)}) copy-start(f32[2,24]{1,0:T(2,128)} %param.16) | copy-start | bytes 580
  99.4 38.3 %collective-permute-start.5 = (bf16[16,96,256]{2,1,0:T(8,128)(2,1)}, bf16[16,96,256]{2,1,0:T(8,128)(2,1)}, u32[]{:S(2)}, u32[]{:S(2)}) collective-permute-start(bf16[16,96,256]{2,1,0:T(8,128)(2,1)} %slice.4), channel_id=1, source_target_pairs={{0,32},{1,33},{2,34},{3,35},{4,36},{5,37},{6,38},{7,39},{32,0},{33... | collective-permute-start | bytes 2359304 | tf_op jit(solution)/shard_map/ppermute | solution.py:41
  104.4 33.3 %collective-permute-start.6 = (bf16[16,96,256]{2,1,0:T(8,128)(2,1)}, bf16[16,96,256]{2,1,0:T(8,128)(2,1)}, u32[]{:S(2)}, u32[]{:S(2)}) collective-permute-start(bf16[16,96,256]{2,1,0:T(8,128)(2,1)} %slice.4), channel_id=1, source_target_pairs={{0,0},{1,1},{2,2},{3,3},{4,4},{5,5},{6,6},{7,7},{32,32},{33,33},{3... | collective-permute-start | bytes 2359304 | tf_op jit(solution)/shard_map/ppermute | solution.py:41
  131.3 0.9 copy-start.7
  132.2 17.1 %all-to-all-start.3 = ((bf16[16,96,256]{2,1,0:T(8,128)(2,1)}), bf16[16,96,256]{2,1,0:T(8,128)(2,1)}, u32[]{:S(2)}, u32[]{:S(2)}) async-start(bf16[16,96,256]{2,1,0:T(8,128)(2,1)} %bitcast.44), calls=%async_computation.3 | async-start | bytes 1572864 | tf_op jit(solution)/shard_map/all_to_all | solution.py:46
  149.3 19.3 %all-to-all-start.4 = ((bf16[16,96,128]{2,1,0:T(8,128)(2,1)}), bf16[16,96,128]{2,1,0:T(8,128)(2,1)S(1)}, u32[]{:S(2)}, u32[]{:S(2)}) async-start(bf16[16,96,128]{2,1,0:T(8,128)(2,1)} %bitcast.16), calls=%async_computation.4 | async-start | bytes 786432 | tf_op jit(solution)/shard_map/all_to_all | solution.py:46
